TPU v7x, 32 devices: a whole 2x2x4 slice. The times are simulated.
32 devices in a mesh: seq: 8 (over z, y), frame: 4 (over x, core).
Axes of the slice: x: 2, y: 2, z: 4, core: 2. Of those that a mesh axis runs over, the one named last changes fastest.
Arguments:
- latents: float32 [24, 64, 1536], P('seq', 'frame'), may hold values from -6 to 6
- patch_feats: float32 [24, 2, 4, 256, 1536], P('seq', None, 'frame'), may hold values from -6 to 6
- image_counts: int32 [24], P('seq'), may hold values from 0 to 8, as said below
- time_index: int32 [24, 8], P('seq'), may hold values from 0 to 7
- query_proj: float32 [1536, 1536], P(('seq', 'frame')), may hold values from -0.15625 to 0.15625
- key_proj: float32 [1536, 1536], P(('seq', 'frame')), may hold values from -0.15625 to 0.15625
- value_proj: float32 [1536, 1536], P(('seq', 'frame')), may hold values from -0.15625 to 0.15625
- out_proj: float32 [1536, 1536], P(('seq', 'frame')), may hold values from -0.625 to 0.625
- up_proj: float32 [1536, 6144], P(('seq', 'frame')), may hold values from -0.15625 to 0.15625
- down_proj: float32 [6144, 1536], P(('seq', 'frame')), may hold values from -0.078125 to 0.078125
- media_gain: float32 [1536], P(('seq', 'frame')), may hold values from 0.1 to 1.9
- media_bias: float32 [1536], P(('seq', 'frame')), may hold values from -4 to 4
- latent_gain: float32 [1536], P(('seq', 'frame')), may hold values from 0.1 to 1.9
- latent_bias: float32 [1536], P(('seq', 'frame')), may hold values from -4 to 4
- feed_gain: float32 [1536], P(('seq', 'frame')), may hold values from 0.1 to 1.9
- feed_bias: float32 [1536], P(('seq', 'frame')), may hold values from -4 to 4
- time_table: float32 [8, 1536], P(None, ('seq', 'frame')), may hold values from -6 to 6
- out_cotangent: float32 [24, 64, 1536], P('seq', 'frame'), may hold values from -6 to 6
Outputs:
- new_latents: float32 [24, 64, 1536], P('seq', 'frame')
- latent_grads: float32 [24, 64, 1536], P('seq', 'frame')
- patch_grads: float32 [24, 2, 4, 256, 1536], P('seq', None, 'frame')
- grad_query: float32 [1536, 1536], P(('seq', 'frame'))
- grad_key: float32 [1536, 1536], P(('seq', 'frame'))
- grad_value: float32 [1536, 1536], P(('seq', 'frame'))
- grad_out: float32 [1536, 1536], P(('seq', 'frame'))
- grad_up: float32 [1536, 6144], P(('seq', 'frame'))
- grad_down: float32 [6144, 1536], P(('seq', 'frame'))
- grad_media_gain: float32 [1536], P(('seq', 'frame'))
- grad_media_bias: float32 [1536], P(('seq', 'frame'))
- grad_latent_gain: float32 [1536], P(('seq', 'frame'))
- grad_latent_bias: float32 [1536], P(('seq', 'frame'))
- grad_feed_gain: float32 [1536], P(('seq', 'frame'))
- grad_feed_bias: float32 [1536], P(('seq', 'frame'))
- grad_time_table: float32 [8, 1536], P(None, ('seq', 'frame'))
Inputs may be any that keep to these rules, and one draw needn't show every extreme that they name: `image_counts`: each aligned block of 3 sequences holds one with 4 images or more, and some sequence has 8.
All inputs are finite; a program needn't handle non-finite values.
Results may differ from a plain program's by a relative error of at most 0.0003.
Values sent between devices are 32-bit elements; how exact they have to be, the bound alone decides.
A program may use at most 512 MiB of HBM per device.

v0:
```python
import functools
import math

import jax
import jax.numpy as jnp
from jax import lax
from jax.experimental import pallas as pl
from jax.experimental.pallas import tpu as pltpu
from jax.sharding import PartitionSpec as P

HEADS = 16


HIGHEST = lax.Precision.HIGHEST
EPSILON = 1e-05
MASKED = -1e30


def product(left, right):
    return jnp.dot(left, right, precision=HIGHEST, preferred_element_type=jnp.float32)


def product_tn(left, right):
    return lax.dot_general(
        left, right, (((0,), (0,)), ((), ())), precision=HIGHEST, preferred_element_type=jnp.float32
    )


def product_nt(left, right):
    return lax.dot_general(
        left, right, (((1,), (1,)), ((), ())), precision=HIGHEST, preferred_element_type=jnp.float32
    )


def flatten(values):
    return values.reshape(-1, values.shape[-1])


def norm_forward(values, gain_vec, bias_vec):
    centred = values - jnp.mean(values, axis=-1, keepdims=True)
    inv_std = lax.rsqrt(jnp.mean(centred * centred, axis=-1, keepdims=True) + EPSILON)
    unit_vals = centred * inv_std
    return (unit_vals * gain_vec + bias_vec, unit_vals, inv_std)


def norm_backward(incoming, unit_vals, inv_std, gain_vec):
    scaled = incoming * gain_vec
    result = inv_std * (
        scaled
        - jnp.mean(scaled, axis=-1, keepdims=True)
        - unit_vals * jnp.mean(scaled * unit_vals, axis=-1, keepdims=True)
    )
    flat_in = flatten(incoming)
    return (result, jnp.sum(flat_in * flatten(unit_vals), axis=0), jnp.sum(flat_in, axis=0))


def heads_last(stats):
    return jnp.transpose(stats, (0, 2, 1))[..., None]


def per_slot(action, operands):
    return lax.map(action, operands)


def body_general(
    latents,
    patch_feats,
    image_counts,
    time_index,
    query_proj,
    key_proj,
    value_proj,
    out_proj,
    up_proj,
    down_proj,
    media_gain,
    media_bias,
    latent_gain,
    latent_bias,
    feed_gain,
    feed_bias,
    time_table,
    out_cotangent,
):
    gathered = (
        lax.all_gather(query_proj, ("seq", "frame"), axis=0, tiled=True),
        lax.all_gather(key_proj, ("seq", "frame"), axis=0, tiled=True),
        lax.all_gather(value_proj, ("seq", "frame"), axis=0, tiled=True),
        lax.all_gather(out_proj, ("seq", "frame"), axis=0, tiled=True),
        lax.all_gather(up_proj, ("seq", "frame"), axis=0, tiled=True),
        lax.all_gather(down_proj, ("seq", "frame"), axis=0, tiled=True),
        lax.all_gather(media_gain, ("seq", "frame"), axis=0, tiled=True),
        lax.all_gather(media_bias, ("seq", "frame"), axis=0, tiled=True),
        lax.all_gather(latent_gain, ("seq", "frame"), axis=0, tiled=True),
        lax.all_gather(latent_bias, ("seq", "frame"), axis=0, tiled=True),
        lax.all_gather(feed_gain, ("seq", "frame"), axis=0, tiled=True),
        lax.all_gather(feed_bias, ("seq", "frame"), axis=0, tiled=True),
        lax.all_gather(time_table, ("seq", "frame"), axis=1, tiled=True),
    )
    gathered = lax.optimization_barrier(gathered)
    (
        query_full,
        key_full,
        value_full,
        out_full,
        up_full,
        down_full,
        mgain_full,
        mbias_full,
        lgain_full,
        lbias_full,
        fgain_full,
        fbias_full,
        table_full,
    ) = gathered
    frame_index = lax.axis_index("frame")
    frame_count = lax.axis_size("frame")
    seq_local, lat_rows, model_width = latents.shape
    round_count = patch_feats.shape[1]
    patch_count = patch_feats.shape[3]
    slot_total = time_index.shape[1]
    table_rows = time_table.shape[0]
    latent_total = lat_rows * frame_count
    head_size = model_width // HEADS
    inv_root = 1.0 / math.sqrt(head_size)
    latent_all = lax.all_gather(latents, "frame", axis=1, tiled=True)
    latent_norm, latent_unit, latent_std = norm_forward(latent_all, lgain_full, lbias_full)
    row_start = frame_index * lat_rows
    own_norm = lax.dynamic_slice_in_dim(latent_norm, row_start, lat_rows, 1)
    own_unit = lax.dynamic_slice_in_dim(latent_unit, row_start, lat_rows, 1)
    own_std = lax.dynamic_slice_in_dim(latent_std, row_start, lat_rows, 1)
    queries = product(flatten(latent_norm), query_full).reshape(
        seq_local, latent_total, model_width
    )
    own_keys = product(flatten(own_norm), key_full).reshape(seq_local, lat_rows, model_width)
    own_values = product(flatten(own_norm), value_full).reshape(seq_local, lat_rows, model_width)
    slot_ids = jnp.arange(round_count, dtype=jnp.int32) * frame_count + frame_index
    present = slot_ids[None, :] < image_counts[:, None]
    picks = jnp.arange(slot_total, dtype=jnp.int32)[None, :] == slot_ids[:, None]
    slot_times = jnp.sum(jnp.where(picks[None, :, :], time_index[:, None, :], 0), axis=-1)
    one_hot = (
        slot_times.reshape(-1)[:, None] == jnp.arange(table_rows, dtype=jnp.int32)[None, :]
    ).astype(jnp.float32)
    slot_embed = product(one_hot, table_full)
    slot_feats = patch_feats.reshape(seq_local * round_count, patch_count, model_width)

    def media_forward(element):
        normed, unit_part, std_part = norm_forward(
            element[0] + element[1][None, :], mgain_full, mbias_full
        )
        return (normed, unit_part, std_part, product(normed, key_full), product(normed, value_full))

    media_norm, media_unit, media_std, media_keys, media_values = per_slot(
        media_forward, (slot_feats, slot_embed)
    )
    key_total = lat_rows + round_count * patch_count
    all_keys = jnp.concatenate(
        [own_keys, media_keys.reshape(seq_local, round_count * patch_count, model_width)], axis=1
    )
    all_values = jnp.concatenate(
        [own_values, media_values.reshape(seq_local, round_count * patch_count, model_width)],
        axis=1,
    )
    keep = jnp.concatenate(
        [jnp.ones((seq_local, lat_rows), dtype=bool), jnp.repeat(present, patch_count, axis=1)],
        axis=1,
    )
    query_four = queries.reshape(seq_local, latent_total, HEADS, head_size)
    key_four = all_keys.reshape(seq_local, key_total, HEADS, head_size)
    value_four = all_values.reshape(seq_local, key_total, HEADS, head_size)

    def masked_scores():
        raw_scores = (
            jnp.einsum(
                "bqhe,bkhe->bhqk",
                query_four,
                key_four,
                precision=HIGHEST,
                preferred_element_type=jnp.float32,
            )
            * inv_root
        )
        return jnp.where(keep[:, None, None, :], raw_scores, MASKED)

    scores = masked_scores()
    row_top = jnp.max(scores, axis=-1)
    expo = jnp.exp(scores - row_top[..., None])
    row_total = jnp.sum(expo, axis=-1)
    partial_out = jnp.einsum(
        "bhqk,bkhe->bqhe", expo, value_four, precision=HIGHEST, preferred_element_type=jnp.float32
    )
    glob_top = lax.pmax(row_top, "frame")
    ratio = jnp.exp(row_top - glob_top)
    glob_total, glob_out = lax.psum((row_total * ratio, partial_out * heads_last(ratio)), "frame")
    attended = glob_out / heads_last(glob_total)
    log_total = glob_top + jnp.log(glob_total)
    attended_flat = attended.reshape(seq_local, latent_total, model_width)
    own_attended = lax.dynamic_slice_in_dim(attended_flat, row_start, lat_rows, 1)
    middle = latents + product(flatten(own_attended), out_full).reshape(
        seq_local, lat_rows, model_width
    )
    feed_norm, feed_unit, feed_std = norm_forward(middle, fgain_full, fbias_full)
    hidden_pre = product(flatten(feed_norm), up_full)
    activated, gelu_pull = jax.vjp(jax.nn.gelu, hidden_pre)
    new_latents = middle + product(activated, down_full).reshape(seq_local, lat_rows, model_width)
    regathered = (
        lax.all_gather(query_proj, ("seq", "frame"), axis=0, tiled=True),
        lax.all_gather(key_proj, ("seq", "frame"), axis=0, tiled=True),
        lax.all_gather(value_proj, ("seq", "frame"), axis=0, tiled=True),
        lax.all_gather(out_proj, ("seq", "frame"), axis=0, tiled=True),
        lax.all_gather(up_proj, ("seq", "frame"), axis=0, tiled=True),
        lax.all_gather(down_proj, ("seq", "frame"), axis=0, tiled=True),
        lax.all_gather(media_gain, ("seq", "frame"), axis=0, tiled=True),
        lax.all_gather(media_bias, ("seq", "frame"), axis=0, tiled=True),
        lax.all_gather(latent_gain, ("seq", "frame"), axis=0, tiled=True),
        lax.all_gather(latent_bias, ("seq", "frame"), axis=0, tiled=True),
        lax.all_gather(feed_gain, ("seq", "frame"), axis=0, tiled=True),
        lax.all_gather(feed_bias, ("seq", "frame"), axis=0, tiled=True),
        lax.all_gather(time_table, ("seq", "frame"), axis=1, tiled=True),
    )
    regathered = lax.optimization_barrier(regathered)
    query_back = regathered[0]
    key_back = regathered[1]
    value_back = regathered[2]
    out_back = regathered[3]
    up_back = regathered[4]
    down_back = regathered[5]
    mgain_back = regathered[6]
    lgain_back = regathered[8]
    fgain_back = regathered[10]
    cotangent = flatten(out_cotangent)
    grad_down = product_tn(activated, cotangent)
    grad_hidden = gelu_pull(product_nt(cotangent, down_back))[0]
    grad_up = product_tn(flatten(feed_norm), grad_hidden)
    grad_feed_norm = product_nt(grad_hidden, up_back).reshape(seq_local, lat_rows, model_width)
    grad_mid_norm, grad_fgain, grad_fbias = norm_backward(
        grad_feed_norm, feed_unit, feed_std, fgain_back
    )
    grad_middle = out_cotangent + grad_mid_norm
    grad_out_w = product_tn(flatten(own_attended), flatten(grad_middle))
    grad_own_att = product_nt(flatten(grad_middle), out_back).reshape(
        seq_local, lat_rows, model_width
    )
    grad_attended = lax.all_gather(grad_own_att, "frame", axis=1, tiled=True)
    grad_four = grad_attended.reshape(seq_local, latent_total, HEADS, head_size)
    delta_rows = jnp.einsum(
        "bqhe,bqhe->bhq", grad_four, attended, precision=HIGHEST, preferred_element_type=jnp.float32
    )
    probs = jnp.exp(masked_scores() - log_total[..., None])
    grad_probs = jnp.einsum(
        "bqhe,bkhe->bhqk",
        grad_four,
        value_four,
        precision=HIGHEST,
        preferred_element_type=jnp.float32,
    )
    grad_scores = probs * (grad_probs - delta_rows[..., None]) * inv_root
    grad_query_part = jnp.einsum(
        "bhqk,bkhe->bqhe",
        grad_scores,
        key_four,
        precision=HIGHEST,
        preferred_element_type=jnp.float32,
    ).reshape(seq_local, latent_total, model_width)
    grad_keys = jnp.einsum(
        "bhqk,bqhe->bkhe",
        grad_scores,
        query_four,
        precision=HIGHEST,
        preferred_element_type=jnp.float32,
    ).reshape(seq_local, key_total, model_width)
    grad_values = jnp.einsum(
        "bhqk,bqhe->bkhe", probs, grad_four, precision=HIGHEST, preferred_element_type=jnp.float32
    ).reshape(seq_local, key_total, model_width)
    grad_query_own = lax.psum_scatter(grad_query_part, "frame", scatter_dimension=1, tiled=True)
    grad_key_lat = flatten(grad_keys[:, :lat_rows])
    grad_value_lat = flatten(grad_values[:, :lat_rows])
    grad_key_media = grad_keys[:, lat_rows:].reshape(
        seq_local * round_count, patch_count, model_width
    )
    grad_value_media = grad_values[:, lat_rows:].reshape(
        seq_local * round_count, patch_count, model_width
    )
    grad_query_w = product_tn(flatten(own_norm), flatten(grad_query_own))
    grad_key_w = product_tn(flatten(own_norm), grad_key_lat) + product_tn(
        flatten(media_norm), flatten(grad_key_media)
    )
    grad_value_w = product_tn(flatten(own_norm), grad_value_lat) + product_tn(
        flatten(media_norm), flatten(grad_value_media)
    )
    grad_own_norm = (
        product_nt(flatten(grad_query_own), query_back)
        + product_nt(grad_key_lat, key_back)
        + product_nt(grad_value_lat, value_back)
    ).reshape(seq_local, lat_rows, model_width)
    grad_lat_in, grad_lgain, grad_lbias = norm_backward(
        grad_own_norm, own_unit, own_std, lgain_back
    )
    latent_grads = grad_middle + grad_lat_in

    def media_backward(element):
        normed_grad = product_nt(element[0], key_back) + product_nt(element[1], value_back)
        feats_grad, gain_part, bias_part = norm_backward(
            normed_grad, element[2], element[3], mgain_back
        )
        return (feats_grad, gain_part, bias_part, jnp.sum(feats_grad, axis=0))

    feats_grads, gain_parts, bias_parts, slot_sums = per_slot(
        media_backward, (grad_key_media, grad_value_media, media_unit, media_std)
    )
    grad_mgain = jnp.sum(gain_parts, axis=0)
    grad_mbias = jnp.sum(bias_parts, axis=0)
    grad_table = product_tn(one_hot, slot_sums)
    patch_grads = feats_grads.reshape(patch_feats.shape)
    (
        grad_query_w,
        grad_key_w,
        grad_value_w,
        grad_out_w,
        grad_up,
        grad_down,
    ) = lax.optimization_barrier(
        (grad_query_w, grad_key_w, grad_value_w, grad_out_w, grad_up, grad_down)
    )
    summed = (
        lax.psum_scatter(grad_query_w, ("seq", "frame"), scatter_dimension=0, tiled=True),
        lax.psum_scatter(grad_key_w, ("seq", "frame"), scatter_dimension=0, tiled=True),
        lax.psum_scatter(grad_value_w, ("seq", "frame"), scatter_dimension=0, tiled=True),
        lax.psum_scatter(grad_out_w, ("seq", "frame"), scatter_dimension=0, tiled=True),
        lax.psum_scatter(grad_up, ("seq", "frame"), scatter_dimension=0, tiled=True),
        lax.psum_scatter(grad_down, ("seq", "frame"), scatter_dimension=0, tiled=True),
        lax.psum_scatter(grad_mgain, ("seq", "frame"), scatter_dimension=0, tiled=True),
        lax.psum_scatter(grad_mbias, ("seq", "frame"), scatter_dimension=0, tiled=True),
        lax.psum_scatter(grad_lgain, ("seq", "frame"), scatter_dimension=0, tiled=True),
        lax.psum_scatter(grad_lbias, ("seq", "frame"), scatter_dimension=0, tiled=True),
        lax.psum_scatter(grad_fgain, ("seq", "frame"), scatter_dimension=0, tiled=True),
        lax.psum_scatter(grad_fbias, ("seq", "frame"), scatter_dimension=0, tiled=True),
        lax.psum_scatter(grad_table, ("seq", "frame"), scatter_dimension=1, tiled=True),
    )
    return (
        new_latents,
        latent_grads,
        patch_grads,
        summed[0],
        summed[1],
        summed[2],
        summed[3],
        summed[4],
        summed[5],
        summed[6],
        summed[7],
        summed[8],
        summed[9],
        summed[10],
        summed[11],
        summed[12],
    )


MESH = pl.DeviceIdType.MESH
F32 = jnp.float32
ANY = pl.BlockSpec(memory_space=pl.ANY)
GRID = (4, 2, 2, 2)


def place(z, y, x, c):
    return (z * 2 + y, x * 2 + c)


class Here:
    def __init__(self):
        seq, frame = lax.axis_index("seq"), lax.axis_index("frame")
        self.z, self.y, self.x, self.c = z, y, x, c = seq // 2, seq % 2, frame // 2, frame % 2
        self.ox, self.oy, self.oc = ox, oy, oc = 1 - x, 1 - y, 1 - c
        self.at_x, self.at_y, self.at_c = place(z, y, ox, c), place(z, oy, x, c), place(z, y, x, oc)
        self.ahead = [lax.rem(z + k, 4) for k in range(4)]
        self.behind = [lax.rem(z + 4 - k, 4) for k in range(4)]
        self.at_z = [place(o, y, x, c) for o in self.ahead]

    def greet(self):
        barrier = pltpu.get_barrier_semaphore()
        for peer in self.at_z[1:] + [self.at_x, self.at_y, self.at_c]:
            pl.semaphore_signal(barrier, inc=1, device_id=peer, device_id_type=MESH)
        pl.semaphore_wait(barrier, 6)


def remote(src, dst, send_sem, recv_sem, peer):
    return pltpu.make_async_remote_copy(
        src_ref=src, dst_ref=dst, send_sem=send_sem, recv_sem=recv_sem, device_id=peer, device_id_type=MESH
    )


class Gather:
    lag = 1

    def __init__(self, here, shards, fulls, cuts, sems):
        self.here, self.count = here, len(cuts)
        self.loc, self.zs, self.zr, self.xs, self.xr, self.ys, self.yr, self.ds, self.dr, self.cs, self.cr = sems
        self.shard = [shards[a].at[:, lo:hi] for a, lo, hi in cuts]
        self.full = [(lambda *at, a=a, lo=lo, hi=hi: fulls[a].at[at + (slice(lo, hi),)]) for a, lo, hi in cuts]
        self.half = [shards[a].shape[0] // 2 for a, lo, hi in cuts]

    @staticmethod
    def semaphores(count):
        dma = pltpu.SemaphoreType.DMA
        shapes = [(), (3,), (3,), (4,), (4,), (4,), (4,), (2, 4), (2, 4), (4,), (4,)]
        return [dma((count,) + s) for s in shapes]

    def local(self, p):
        h = self.here
        return pltpu.make_async_copy(self.shard[p], self.full[p](h.z, h.y, h.x, h.c, slice(None)), self.loc.at[p])

    def over_z(self, p, k):
        h = self.here
        dst = self.full[p](h.z, h.y, h.x, h.c, slice(None))
        return remote(self.shard[p], dst, self.zs.at[p, k - 1], self.zr.at[p, k - 1], h.at_z[k])

    def over_x(self, p, k):
        h = self.here
        block = self.full[p](h.behind[k], h.y, h.x, h.c, slice(None))
        return remote(self.shard[p] if k == 0 else block, block, self.xs.at[p, k], self.xr.at[p, k], h.at_x)

    def over_y(self, p, k):
        h = self.here
        block = self.full[p](h.behind[k], h.y, h.x, h.c, slice(None))
        return remote(self.shard[p] if k == 0 else block, block, self.ys.at[p, k], self.yr.at[p, k], h.at_y)

    def on_y(self, p, k):
        h = self.here
        part = self.full[p](h.behind[k], h.y, h.ox, h.c, slice(self.half[p], 2 * self.half[p]))
        return remote(part, part, self.ds.at[p, 0, k], self.dr.at[p, 0, k], h.at_y)

    def on_x(self, p, k):
        h = self.here
        part = self.full[p](h.behind[k], h.oy, h.x, h.c, slice(0, self.half[p]))
        return remote(part, part, self.ds.at[p, 1, k], self.dr.at[p, 1, k], h.at_x)

    def to_core(self, p, i):
        h = self.here
        yy, xx = ((h.y, h.x), (h.y, h.ox), (h.oy, h.x), (h.oy, h.ox))[i]
        blocks = self.full[p](slice(None), yy, xx, h.c, slice(None))
        return remote(blocks, blocks, self.cs.at[p, i], self.cr.at[p, i], h.at_c)

    def own(self, p):
        self.local(p).start()
        for k in (1, 2, 3):
            self.over_z(p, k).start()
        self.over_x(p, 0).start()
        self.over_y(p, 0).start()

    def along_z(self, p):
        for k in (1, 2, 3):
            self.over_z(p, k).wait_recv()
            self.over_x(p, k).start()
            self.over_y(p, k).start()

    def across(self, p):
        for k in range(4):
            self.over_x(p, k).wait_recv()
            self.on_y(p, k).start()
            self.over_y(p, k).wait_recv()
            self.on_x(p, k).start()
        self.local(p).wait()
        for i in range(3):
            self.to_core(p, i).start()

    def corner(self, p):
        for k in range(4):
            self.on_y(p, k).wait_recv()
            self.on_x(p, k).wait_recv()
        self.to_core(p, 3).start()

    def arrived(self, p):
        for i in range(4):
            self.to_core(p, i).wait_recv()

    def done(self, p, here=False):
        if not here:
            self.arrived(p)
        for i in range(4):
            self.to_core(p, i).wait_send()
        for k in (1, 2, 3):
            self.over_z(p, k).wait_send()
        for k in range(4):
            for copy in (self.over_x, self.over_y, self.on_x, self.on_y):
                copy(p, k).wait_send()

    def stages(self):
        return (self.own, self.along_z, self.across, self.corner)


LAG = 2


def waves_of(plan, ahead):
    first, *stages = plan.stages()
    count, last, lag = plan.count, len(stages) - 1, plan.lag
    ahead = min(ahead, count)
    waves = [[functools.partial(first, p) for p in range(ahead)]]
    for t in range(count + last * lag):
        wave = [functools.partial(first, t + ahead)] if t + ahead < count else []
        order = range(last, -1, -1)
        waves.append(wave + [functools.partial(stages[s], t - s * lag) for s in order if 0 <= t - s * lag < count])
    return waves


def finish_all(plan):
    for p in range(plan.count):
        plan.done(p)


class Scatter:
    lag = LAG

    def __init__(self, here, count, mine, theirs, load, out, scratch):
        self.here, self.count, self.mine, self.theirs, self.load, self.out = here, count, mine, theirs, load, out
        self.got, self.gx, self.gy, self.hx, self.hy, self.gz = scratch[:6]
        self.cs, self.cr, self.fs, self.fr, self.ss, self.sr, self.zs, self.zr = scratch[6:]
        self.half = self.got.shape[-2] // 2

    @staticmethod
    def scratch(count, r, w):
        dma = pltpu.SemaphoreType.DMA
        leads = [(4, 2, 2, r), (4, 2, r // 2), (4, 2, r // 2), (4, r // 2), (4, r // 2), (3, r)]
        return [pltpu.VMEM((count,) + s + (w,), F32) for s in leads] + [
            dma((count,) + s) for s in ((), (), (2,), (2,), (2,), (2,), (3,), (3,))
        ]

    def to_core(self, p):
        return remote(self.theirs(p), self.got.at[p], self.cs.at[p], self.cr.at[p], self.here.at_c)

    def first(self, p, way):
        h, half, tot = self.here, self.half, self.mine(p)
        if way == 0:
            return remote(tot.at[:, :, h.ox, :half], self.gx.at[p], self.fs.at[p, 0], self.fr.at[p, 0], h.at_x)
        return remote(tot.at[:, h.oy, :, half:], self.gy.at[p], self.fs.at[p, 1], self.fr.at[p, 1], h.at_y)

    def second(self, p, way):
        h, half, tot = self.here, self.half, self.mine(p)
        if way == 0:
            return remote(tot.at[:, h.oy, h.x, :half], self.hy.at[p], self.ss.at[p, 0], self.sr.at[p, 0], h.at_y)
        return remote(tot.at[:, h.y, h.ox, half:], self.hx.at[p], self.ss.at[p, 1], self.sr.at[p, 1], h.at_x)

    def over_z(self, p, k):
        h = self.here
        src = self.mine(p).at[h.ahead[k], h.y, h.x]
        return remote(src, self.gz.at[p, k - 1], self.zs.at[p, k - 1], self.zr.at[p, k - 1], h.at_z[k])

    def start(self, p):
        if self.load is not None:
            self.load(p).start()
        self.to_core(p).start()

    def cores(self, p):
        tot, got = self.mine(p), self.got.at[p]
        if self.load is not None:
            self.load(p).wait()
        self.to_core(p).wait_recv()

        @pl.loop(0, 16)
        def _(i):
            at = (i // 4, (i // 2) % 2, i % 2)
            tot[at] = tot[at] + got[at]

        self.first(p, 0).start()
        self.first(p, 1).start()

    def sides(self, p):
        h, half, tot = self.here, self.half, self.mine(p)
        gx, gy = self.gx.at[p], self.gy.at[p]
        self.first(p, 0).wait_recv()

        @pl.loop(0, 8)
        def _(i):
            zi, yi = i // 2, i % 2
            tot[zi, yi, h.x, :half] = tot[zi, yi, h.x, :half] + gx[zi, yi]

        self.second(p, 0).start()
        self.first(p, 1).wait_recv()

        @pl.loop(0, 8)
        def _(i):
            zi, xi = i // 2, i % 2
            tot[zi, h.y, xi, half:] = tot[zi, h.y, xi, half:] + gy[zi, xi]

        self.second(p, 1).start()

    def column(self, p):
        h, half, tot = self.here, self.half, self.mine(p)
        hx, hy = self.hx.at[p], self.hy.at[p]
        self.second(p, 0).wait_recv()
        self.second(p, 1).wait_recv()

        @pl.loop(0, 4)
        def _(zi):
            tot[zi, h.y, h.x, :half] = tot[zi, h.y, h.x, :half] + hy[zi]
            tot[zi, h.y, h.x, half:] = tot[zi, h.y, h.x, half:] + hx[zi]

        for k in (1, 2, 3):
            self.over_z(p, k).start()

    def finish(self, p):
        h, gz = self.here, self.gz.at[p]
        for k in (1, 2, 3):
            self.over_z(p, k).wait_recv()
        self.out(p)[...] = (self.mine(p)[h.z, h.y, h.x] + gz[0]) + (gz[1] + gz[2])

    def done(self, p):
        self.to_core(p).wait_send()
        for way in (0, 1):
            self.first(p, way).wait_send()
            self.second(p, way).wait_send()
        for k in (1, 2, 3):
            self.over_z(p, k).wait_send()

    def stages(self):
        return (self.start, self.cores, self.sides, self.column, self.finish)


def run(wave):
    for action in wave:
        action()


class Pace:
    def __init__(self, step, steps, lead, parts, waves):
        self.step, self.steps, self.lead, self.parts = step, steps, lead, parts
        ticks, total, before = lead + steps * parts, 1 + sum(len(w) for w in waves[1:]), 0
        self.waves = [[] for _ in range(ticks)]
        for wave in waves:
            self.waves[ticks * before // total] += wave
            before += len(wave) if before else 1

    def at_lead(self, i):
        run(self.waves[i])

    def at(self, part):
        for s in range(self.steps):
            now = self.waves[self.lead + s * self.parts + part]
            if now:
                pl.when(self.step == s)(functools.partial(run, now))


def run_last(step, steps, plan):
    @pl.when(step == steps - 1)
    def _():
        finish_all(plan)


WIDE = 768


def column_cuts(shards):
    return [(a, lo, min(lo + WIDE, s.shape[1])) for a, s in enumerate(shards) for lo in range(0, s.shape[1], WIDE)]


class GroupGather:
    def __init__(self, here, shards, fulls, sems):
        self.here, self.shards, self.fulls, self.count = here, shards, fulls, len(shards)
        self.loc, self.ss, self.rs = sems

    @staticmethod
    def semaphores(count):
        dma = pltpu.SemaphoreType.DMA
        return [dma((count,)), dma((count, 3)), dma((count, 3))]

    def local(self, a):
        h = self.here
        return pltpu.make_async_copy(self.shards[a], self.fulls[a].at[:, h.x * 2 + h.c], self.loc.at[a])

    def copy(self, a, i):
        h = self.here
        mine = self.fulls[a].at[:, h.x * 2 + h.c]
        if i < 2:
            return remote(self.shards[a], mine, self.ss.at[a, i], self.rs.at[a, i], (h.at_x, h.at_c)[i])
        block = self.fulls[a].at[:, h.ox * 2 + h.c]
        return remote(block, block, self.ss.at[a, 2], self.rs.at[a, 2], h.at_c)

    def start(self):
        for a in range(self.count):
            self.local(a).start()
            self.copy(a, 0).start()
            self.copy(a, 1).start()

    def forward(self):
        for a in range(self.count):
            self.copy(a, 0).wait_recv()
            self.copy(a, 2).start()

    def done(self):
        for a in range(self.count):
            self.local(a).wait()
            self.copy(a, 0).wait_send()
            self.copy(a, 1).wait()
            self.copy(a, 2).wait()


def flat_full(full):
    return full.reshape((-1, full.shape[-1]))


def full_shapes(shards):
    return [jax.ShapeDtypeStruct(GRID + s.shape, s.dtype) for s in shards]


def gather_kernel(count, cuts, *refs):
    here = Here()
    here.greet()
    plan = Gather(here, refs[:count], refs[count : 2 * count], cuts, refs[2 * count :])
    for wave in waves_of(plan, 2):
        run(wave)
    finish_all(plan)


def gather_all(shards, collective_id):
    count = len(shards)
    cuts = column_cuts(shards)
    outs = pl.pallas_call(
        functools.partial(gather_kernel, count, cuts),
        out_shape=full_shapes(shards),
        in_specs=[ANY] * count,
        out_specs=[ANY] * count,
        scratch_shapes=Gather.semaphores(len(cuts)),
        compiler_params=pltpu.CompilerParams(collective_id=collective_id, has_side_effects=True),
        name="gather_all",
    )(*shards)
    return [flat_full(o) for o in outs]


class Summed:
    def __init__(self, parts):
        self.arrays = len(parts)
        self.rows, self.width = parts[0].shape[0] // 32, parts[0].shape[1]
        self.cut = min(256, self.width)
        self.pieces = self.width // self.cut
        self.operands = [p.reshape(GRID + (self.rows, self.width)) for p in parts]
        self.in_specs = [ANY] * len(parts)
        self.out_shape = [jax.ShapeDtypeStruct((self.rows, self.width), F32)] * len(parts)
        self.out_specs = [whole((self.rows, self.width))] * len(parts)
        n = self.count = len(parts) * self.pieces
        self.scratch = [pltpu.VMEM((n, 4, 2, 2, self.rows, self.cut), F32), pltpu.SemaphoreType.DMA((n,))]
        self.scratch += Scatter.scratch(n, self.rows, self.cut)

    def bind(self, here, ins, outs, scratch):
        tots, loc = scratch[:2]

        def cut(p):
            lo = p % self.pieces * self.cut
            return p // self.pieces, slice(lo, lo + self.cut)

        def part(p, core):
            a, cols = cut(p)
            return ins[a].at[:, :, :, core, :, cols]

        def out(p):
            a, cols = cut(p)
            return outs[a].at[:, cols]

        return Scatter(
            here,
            self.count,
            lambda p: tots.at[p],
            lambda p: part(p, here.oc),
            lambda p: pltpu.make_async_copy(part(p, here.c), tots.at[p], loc.at[p]),
            out,
            scratch[2:],
        )


def scatter_kernel(plan, *refs):
    n = plan.arrays
    here = Here()
    here.greet()
    sums = plan.bind(here, refs[:n], refs[n : 2 * n], refs[2 * n :])
    for wave in waves_of(sums, sums.count):
        run(wave)
    finish_all(sums)


def scatter_all(parts, collective_id):
    plan = Summed(parts)
    return pl.pallas_call(
        functools.partial(scatter_kernel, plan),
        out_shape=plan.out_shape,
        in_specs=plan.in_specs,
        out_specs=[pl.BlockSpec(memory_space=pltpu.VMEM)] * len(parts),
        scratch_shapes=plan.scratch,
        compiler_params=pltpu.CompilerParams(
            collective_id=collective_id, has_side_effects=True, vmem_limit_bytes=60 * 2**20
        ),
        name="scatter_all",
    )(*plan.operands)


def greet(peers):
    barrier = pltpu.get_barrier_semaphore()
    for peer in peers:
        pl.semaphore_signal(barrier, inc=1, device_id=peer, device_id_type=MESH)
    pl.semaphore_wait(barrier, len(peers))


def group_gather_kernel(count, *refs):
    shards, fulls = refs[:count], refs[count : 2 * count]
    loc, ss, rs = refs[2 * count :]
    here = Here()
    x, c, ox, at_x, at_c = here.x, here.c, here.ox, here.at_x, here.at_c
    greet([at_x, at_c])
    waits = []
    for a in range(count):
        mine = fulls[a].at[:, x * 2 + c]
        copy = pltpu.make_async_copy(shards[a], mine, loc.at[a])
        copy.start()
        over = remote(shards[a], mine, ss.at[a, 0], rs.at[a, 0], at_x)
        over.start()
        side = remote(shards[a], mine, ss.at[a, 1], rs.at[a, 1], at_c)
        side.start()
        waits.append((copy, over, side))
    last = []
    for a in range(count):
        waits[a][1].wait_recv()
        block = fulls[a].at[:, ox * 2 + c]
        on = remote(block, block, ss.at[a, 2], rs.at[a, 2], at_c)
        on.start()
        last.append(on)
    for a in range(count):
        copy, over, side = waits[a]
        copy.wait()
        over.wait_send()
        side.wait()
        last[a].wait()


def group_gather(shards, collective_id):
    count = len(shards)
    dma = pltpu.SemaphoreType.DMA
    return pl.pallas_call(
        functools.partial(group_gather_kernel, count),
        out_shape=[jax.ShapeDtypeStruct((s.shape[0], 4) + s.shape[1:], F32) for s in shards],
        in_specs=[ANY] * count,
        out_specs=[ANY] * count,
        scratch_shapes=[dma((count,)), dma((count, 3)), dma((count, 3))],
        compiler_params=pltpu.CompilerParams(collective_id=collective_id, has_side_effects=True),
        name="group_gather",
    )(*shards)


def group_swap_kernel(count, *refs):
    shards, fulls = refs[:count], refs[count : 2 * count]
    loc, ss, rs = refs[2 * count :]
    here = Here()
    z, y, x, c = here.z, here.y, here.x, here.c
    me = x * 2 + c
    peers = [(x, 1 - c), (1 - x, c), (1 - x, 1 - c)]
    greet([place(z, y, *p) for p in peers])
    waits = []
    for a in range(count):
        copy = pltpu.make_async_copy(shards[a].at[:, me], fulls[a].at[:, me], loc.at[a])
        copy.start()
        waits.append(copy)
        for k in (1, 2, 0):
            px, pc = peers[k]
            on = remote(
                shards[a].at[:, px * 2 + pc], fulls[a].at[:, me], ss.at[a, k], rs.at[a, k], place(z, y, px, pc)
            )
            on.start()
            waits.append(on)
    for copy in waits:
        copy.wait()


def group_swap(shards, collective_id):
    count = len(shards)
    dma = pltpu.SemaphoreType.DMA
    return pl.pallas_call(
        functools.partial(group_swap_kernel, count),
        out_shape=[jax.ShapeDtypeStruct(s.shape, F32) for s in shards],
        in_specs=[ANY] * count,
        out_specs=[ANY] * count,
        scratch_shapes=[dma((count,)), dma((count, 3)), dma((count, 3))],
        compiler_params=pltpu.CompilerParams(collective_id=collective_id, has_side_effects=True),
        name="group_swap",
    )(*shards)


BF16 = jnp.bfloat16
HIGH = lax.Precision.HIGH
BLOCK = 256


def dot(left, right, dims=(1, 0)):
    return lax.dot_general(
        left, right, (((dims[0],), (dims[1],)), ((), ())), precision=HIGH, preferred_element_type=F32
    )


def dot3(left, right, dims=(1, 0)):
    numbers = (((dims[0],), (dims[1],)), ((), ()))
    one = functools.partial(lax.dot_general, dimension_numbers=numbers, preferred_element_type=F32)
    return one(left[0], right[0]) + (one(left[0], right[1]) + one(left[1], right[0]))


def halves(values):
    top = values.astype(BF16)
    return top, (values - top.astype(F32)).astype(BF16)


def split_weights(sources, pairs, stage, sems, pace):
    step = stage.shape[1]
    chunks = [(i, r) for i, s in enumerate(sources) for r in range(0, s.shape[0], step)]

    def copy(n):
        i, r = chunks[n]
        return pltpu.make_async_copy(sources[i].at[r : r + step], stage.at[n % 2], sems.at[n % 2])

    copy(0).start()
    for n, (i, r) in enumerate(chunks):
        if n * pace.lead % len(chunks) == 0:
            pace.at_lead(n * pace.lead // len(chunks))
        if n + 1 < len(chunks):
            copy(n + 1).start()
        copy(n).wait()
        pairs[i][0][r : r + step], pairs[i][1][r : r + step] = halves(stage[n % 2])


def unit_of(values):
    centred = values - jnp.mean(values, axis=-1, keepdims=True)
    inv_std = lax.rsqrt(jnp.mean(centred * centred, axis=-1, keepdims=True) + EPSILON)
    return centred * inv_std, inv_std


def staging(width):
    return [pltpu.VMEM((width, width), BF16)] * 4 + [pltpu.VMEM((2, 128, width), F32), pltpu.SemaphoreType.DMA((2,))]


def whole(shape, buffers=1):
    return pl.BlockSpec(shape, lambda *i: (0,) * len(shape), pipeline_mode=pl.Buffered(buffers))


def opening_kernel(cuts, *refs):
    times, feats, latents = refs[:3]
    shards, group_shard = refs[3:9], refs[9:10]
    vec, keys, values, own_keys, own_values, queries, xt_top, xt_low = refs[10:18]
    fulls, group_full = refs[18:24], refs[24:25]
    pk, top, low, own_top, own_low, lat, lat_top, lat_low, stage, load = refs[25:35]
    step = pl.program_id(0)
    here = Here()
    vectors = Gather(here, shards[:1], fulls[:1], [(0, 0, 128)], refs[35:46])
    moved = Gather(here, shards[1:], fulls[1:], cuts, refs[46:57])
    group = GroupGather(here, group_shard, group_full, refs[57:])
    waves = waves_of(moved, 2)
    cut = keys.shape[1]
    slots, chunks = top.shape[0] // BLOCK, shards[1].shape[1] // cut

    def start():
        here.greet()
        vectors.own(0)
        run(waves[0])
        group.start()
        vectors.along_z(0)
        vectors.across(0)
        vectors.corner(0)
        vectors.arrived(0)
        copy = pltpu.make_async_copy(fulls[0], pk, load.at[0])
        copy.start()
        copy.wait()
        strip = shards[1].shape[0]
        vec[...] = jnp.concatenate([pk[i // 8, i // 4 % 2, i // 2 % 2, i % 2][:, :strip] for i in range(32)], axis=1)
        own_top[...], own_low[...] = halves(unit_of(latents[...])[0] * vec[2:3] + vec[3:4])
        run(waves[1])
        group.forward()

    pl.when(step == 0)(start)
    at_step = {2: 2, 4: 3, 5: 4, slots + 1: 5, slots + 2: 6, slots + 4: 7, slots + 5: 8}
    at_step.update({slots + chunks + i: 8 + i for i in range(1, 5)})
    for s, w in at_step.items():
        pl.when(step == s)(functools.partial(run, waves[w]))

    @pl.when(step < slots)
    def _():
        embed = vec[pl.ds(6 + times[step], 1)]
        normed = unit_of(feats[...] + embed)[0] * vec[0:1] + vec[1:2]
        rows = pl.ds(pl.multiple_of(step * BLOCK, BLOCK), BLOCK)
        top[rows], low[rows] = halves(normed)
        xt_top[...], xt_low[...] = halves(jnp.swapaxes(normed, 0, 1))

    def chunk(array, n, left, right, out, own_out):
        cols = pl.ds(pl.multiple_of(n * cut, cut), cut)
        copy = pltpu.make_async_copy(fulls[array].at[:, :, :, :, :, cols], stage.at[array % 2], load.at[0])
        copy.start()
        copy.wait()
        pair = halves(stage[array % 2].reshape((-1, cut)))
        step_rows = min(512, left.shape[0])

        @pl.loop(0, left.shape[0] // step_rows)
        def _(m):
            rows = pl.ds(pl.multiple_of(m * step_rows, step_rows), step_rows)
            out[rows] = dot3((left[rows], right[rows]), pair)

        if own_out is not None:
            own_out[...] = dot3((own_top[...], own_low[...]), pair)

    half = chunks // 2
    for first in (0, 1):

        @pl.when(step == slots + first * half)
        def _():
            moved.arrived(2 * first)
            moved.arrived(2 * first + 1)

    @pl.when((step >= slots) & (step < slots + chunks))
    def _():
        chunk(1, step - slots, top, low, keys, own_keys)
        chunk(2, step - slots, top, low, values, own_values)

    @pl.when(step == slots + chunks)
    def _():
        moved.arrived(4)
        moved.arrived(5)
        group.done()
        copy = pltpu.make_async_copy(group_full[0], lat, load.at[0])
        copy.start()
        copy.wait()
        lat_top[...], lat_low[...] = halves(unit_of(lat[...].reshape(lat_top.shape))[0] * vec[2:3] + vec[3:4])

    @pl.when(step >= slots + chunks)
    def _():
        chunk(3, step - slots - chunks, lat_top, lat_low, queries, None)

    @pl.when(step == slots + 2 * chunks - 1)
    def _():
        vectors.done(0, True)
        for p in range(moved.count):
            moved.done(p, p < 6)


def opening(times, feats, latents, packed, key_w, value_w, query_w, cot, out_w, collective_id):
    rows, width = feats.shape
    seqs, own_each, _ = latents.shape
    own_rows, lat_rows = seqs * own_each, seqs * own_each * 4
    slots, cut = rows // BLOCK, 256
    chunks = width // cut
    shards = [packed, key_w, value_w, query_w, cot, out_w]
    cuts = [(a, lo, lo + WIDE) for lo in range(0, width, WIDE) for a in (0, 1)]
    cuts += [(a, lo, lo + WIDE) for a in (2, 3, 4) for lo in range(0, width, WIDE)]
    clip = lambda i, lo: jnp.clip(i - lo, 0, chunks - 1)
    chunk_of = lambda n, lo: pl.BlockSpec((n, cut), lambda i: (0, clip(i, lo)))
    turned = pl.BlockSpec((width, BLOCK), lambda i: (0, jnp.minimum(i, slots - 1)))
    full = lambda n, kind=F32: jax.ShapeDtypeStruct((n, width), kind)
    outs = pl.pallas_call(
        functools.partial(opening_kernel, cuts),
        grid=(slots + 2 * chunks,),
        in_specs=[
            SMEM,
            pl.BlockSpec((BLOCK, width), lambda i: (jnp.minimum(i, slots - 1), 0)),
            whole((own_rows, width)),
        ]
        + [ANY] * 7,
        out_specs=[
            whole((16, width)),
            chunk_of(rows, slots),
            chunk_of(rows, slots),
            chunk_of(own_rows, slots),
            chunk_of(own_rows, slots),
            chunk_of(lat_rows, slots + chunks),
            turned,
            turned,
        ]
        + [ANY] * 7,
        out_shape=[full(16), full(rows), full(rows), full(own_rows), full(own_rows), full(lat_rows)]
        + [jax.ShapeDtypeStruct((width, rows), BF16)] * 2
        + full_shapes(shards)
        + [jax.ShapeDtypeStruct((seqs, 4, own_each, width), F32)],
        scratch_shapes=[
            pltpu.VMEM(GRID + packed.shape, F32),
            pltpu.VMEM((rows, width), BF16),
            pltpu.VMEM((rows, width), BF16),
            pltpu.VMEM((own_rows, width), BF16),
            pltpu.VMEM((own_rows, width), BF16),
            pltpu.VMEM((seqs, 4, own_each, width), F32),
            pltpu.VMEM((lat_rows, width), BF16),
            pltpu.VMEM((lat_rows, width), BF16),
            pltpu.VMEM((2,) + GRID + (width // 32, cut), F32),
            pltpu.SemaphoreType.DMA((1,)),
        ]
        + Gather.semaphores(1)
        + Gather.semaphores(len(cuts))
        + GroupGather.semaphores(1),
        compiler_params=pltpu.CompilerParams(
            collective_id=collective_id, has_side_effects=True, vmem_limit_bytes=60 * 2**20
        ),
        name="opening",
    )(times, feats, latents.reshape(own_rows, width), *shards, latents)
    return outs[:8], [flat_full(o) for o in outs[9:14]], outs[14]


def pair_rows(values, first, head):
    lane = lax.broadcasted_iota(jnp.int32, values.shape, 1)
    return jnp.concatenate(
        [
            jnp.where((lane >= first) & (lane < first + head), values, 0.0),
            jnp.where((lane >= first + head) & (lane < first + 2 * head), values, 0.0),
        ],
        axis=0,
    )


def pair_merge(stacked, first, head):
    half = stacked.shape[0] // 2
    lane = lax.broadcasted_iota(jnp.int32, (half, stacked.shape[1]), 1)
    one = jnp.where((lane >= first) & (lane < first + head), stacked[:half], 0.0)
    return one + jnp.where((lane >= first + head) & (lane < first + 2 * head), stacked[half:], 0.0)


def join(left, right):
    return jnp.concatenate([left[:, :128], left[:, 128:] + right[:, :128], right[:, 128:]], axis=1)


def windows(head):
    return ((slice(0, 256), 0), (slice(128, 384), 2 * head - 128))


def score_block(present, seq, keys, own_keys, q_pair, window, inv_root):
    at = keys.shape[0]
    scores = jnp.concatenate([dot(keys[:, window], q_pair, (1, 1)), dot(own_keys[:, window], q_pair, (1, 1))], axis=0)
    row = lax.broadcasted_iota(jnp.int32, scores.shape, 0)
    keep = (row >= at) | ((row < at // 2) & (present[seq, 0] > 0)) | ((row >= at // 2) & (present[seq, 1] > 0))
    return jnp.where(keep, scores * inv_root, MASKED)


def attend_kernel(inv_root, head, present, queries, keys, values, own_keys, own_values, out, tops, sums):
    seq, group = pl.program_id(0), pl.program_id(1)
    merged = []
    for p, (window, first) in enumerate(windows(head)):
        q_pair = pair_rows(queries[:, window], first, head)
        scores = score_block(present, seq, keys, own_keys, q_pair, window, inv_root)
        top = jnp.max(scores, axis=0, keepdims=True)
        expo = jnp.exp(scores - top)
        tops[pl.ds(group * 2 + p, 1)] = top
        sums[pl.ds(group * 2 + p, 1)] = jnp.sum(expo, axis=0, keepdims=True)
        at = keys.shape[0]
        stacked = dot(expo[:at], values[:, window], (0, 0)) + dot(expo[at:], own_values[:, window], (0, 0))
        merged.append(pair_merge(stacked, first, head))
    out[...] = join(*merged)


def attend_specs(lat, media, rows):
    group = 384
    query = pl.BlockSpec((None, lat, group), lambda b, g: (b, 0, g))
    key = pl.BlockSpec((media, group), lambda b, g: (b, g))
    own = pl.BlockSpec((rows, group), lambda b, g: (b, g))
    stat = pl.BlockSpec((None, 8, 128), lambda b, g: (b, 0, 0))
    return query, key, own, stat


SMEM = pl.BlockSpec(memory_space=pltpu.SMEM)


def attend(present, queries, keys, values, own_keys, own_values):
    seqs, lat, width = queries.shape
    head = width // HEADS
    query, key, own, stat = attend_specs(lat, keys.shape[0] // seqs, own_keys.shape[0] // seqs)
    stat_shape = jax.ShapeDtypeStruct((seqs, 8, 128), F32)
    return pl.pallas_call(
        functools.partial(attend_kernel, 1.0 / math.sqrt(head), head),
        grid=(seqs, width // 384),
        in_specs=[SMEM, query, key, key, own, own],
        out_specs=[query, stat, stat],
        out_shape=[jax.ShapeDtypeStruct(queries.shape, F32), stat_shape, stat_shape],
        compiler_params=pltpu.CompilerParams(vmem_limit_bytes=60 * 2**20),
        name="attend",
    )(present, queries, keys, values, own_keys, own_values)


def attend_back_kernel(inv_root, head, plan, steps, *refs):
    present, queries, grads, logs, deltas, keys, values, own_keys, own_values = refs[:9]
    n = plan.arrays
    query_out, key_out, value_out, own_key_out, own_value_out = refs[9 + n : 14 + n]
    seq, group = pl.program_id(0), pl.program_id(1)
    step = seq * pl.num_programs(1) + group
    here = Here()
    moved = plan.bind(here, refs[9 : 9 + n], refs[14 + n : 14 + 2 * n], refs[14 + 2 * n :])
    waves = waves_of(moved, moved.count)
    waves[0].insert(0, here.greet)
    pace = Pace(step, steps, 0, 2, waves)
    merged, key_grads, value_grads = [], [], []
    at = keys.shape[0]
    for p, (window, first) in enumerate(windows(head)):
        pace.at(p)
        q_pair = pair_rows(queries[:, window], first, head)
        g_pair = pair_rows(grads[:, window], first, head)
        scores = score_block(present, seq, keys, own_keys, q_pair, window, inv_root)
        probs = jnp.exp(scores - logs[pl.ds(group * 2 + p, 1)])
        grad_probs = jnp.concatenate(
            [dot(values[:, window], g_pair, (1, 1)), dot(own_values[:, window], g_pair, (1, 1))], axis=0
        )
        grad_scores = probs * (grad_probs - deltas[pl.ds(group * 2 + p, 1)]) * inv_root
        stacked = dot(grad_scores[:at], keys[:, window], (0, 0)) + dot(grad_scores[at:], own_keys[:, window], (0, 0))
        merged.append(pair_merge(stacked, first, head))
        key_grads.append(dot(grad_scores, q_pair))
        value_grads.append(dot(probs, g_pair))
    query_out[...] = join(*merged)
    key_grad, value_grad = join(*key_grads), join(*value_grads)
    key_out[...], own_key_out[...] = key_grad[:at], key_grad[at:]
    value_out[...], own_value_out[...] = value_grad[:at], value_grad[at:]
    run_last(step, steps, moved)


def attend_back(present, queries, grads, logs, deltas, keys, values, own_keys, own_values, plan, collective_id):
    seqs, lat, width = queries.shape
    head = width // HEADS
    query, key, own, stat = attend_specs(lat, keys.shape[0] // seqs, own_keys.shape[0] // seqs)
    shape = lambda v: jax.ShapeDtypeStruct(v.shape, F32)
    grid = (seqs, width // 384)
    outs = pl.pallas_call(
        functools.partial(attend_back_kernel, 1.0 / math.sqrt(head), head, plan, grid[0] * grid[1]),
        grid=grid,
        in_specs=[SMEM, query, query, stat, stat, key, key, own, own] + plan.in_specs,
        out_specs=[query, key, key, own, own] + plan.out_specs,
        out_shape=[shape(queries), shape(keys), shape(values), shape(own_keys), shape(own_values)] + plan.out_shape,
        scratch_shapes=plan.scratch,
        compiler_params=pltpu.CompilerParams(
            collective_id=collective_id, has_side_effects=True, vmem_limit_bytes=60 * 2**20
        ),
        name="attend_back",
    )(present, queries, grads, logs, deltas, keys, values, own_keys, own_values, *plan.operands)
    return outs[:5], outs[5:]


def weight_kernel(steps, xt_top, xt_low, own_t, grad_keys, grad_values, own_gk, own_gv, vec, outs, vec_out, mats, *rest):
    n = pl.program_id(0)
    here = Here()
    cut = grad_keys.shape[1]
    sums = Scatter(
        here,
        2 * steps,
        lambda p: mats.at[p, :, :, :, here.c],
        lambda p: mats.at[p, :, :, :, here.oc],
        None,
        lambda p: outs.at[p % 2, :, pl.ds(pl.multiple_of(p // 2 * cut, cut), cut)],
        rest[:14],
    )
    tot, loc = rest[14:16]
    small = Scatter(
        here,
        1,
        lambda p: tot,
        lambda p: vec.at[:, :, :, here.oc],
        lambda p: pltpu.make_async_copy(vec.at[:, :, :, here.c], tot, loc.at[p]),
        lambda p: vec_out,
        rest[16:],
    )
    stages = sums.stages()

    @pl.when(n == 0)
    def _():
        here.greet()

    for w, (grad, own_grad) in enumerate(((grad_keys, own_gk), (grad_values, own_gv))):
        pair = halves(grad[...])
        top, low = halves(own_grad[...])
        stacked = jnp.concatenate([top, low, top], axis=0)

        @pl.loop(0, 2)
        def _(i):
            rows = pl.ds(pl.multiple_of(i * 768, 768), 768)
            made = dot3((xt_top[rows], xt_low[rows]), pair)
            made += jnp.dot(own_t[rows], stacked, preferred_element_type=F32)
            mats[2 * n + w, pl.ds(i * 2, 2)] = made.reshape((2, 2, 2, 2, 48, cut))

        sums.start(2 * n + w)
        for s in (4, 3, 2, 1):
            p = 2 * n + w - LAG * s

            @pl.when(p >= 0)
            def _():
                stages[s](p)

        if w == 1:
            for s in range(5):

                @pl.when(n == s)
                def _():
                    small.stages()[s](0)

    @pl.when(n == steps - 1)
    def _():
        for t in range(2 * steps, 2 * steps + 4 * LAG):
            for s in (4, 3, 2, 1):
                if 0 <= t - LAG * s < 2 * steps:
                    stages[s](t - LAG * s)

        @pl.loop(0, 2 * steps)
        def _(p):
            sums.done(p)

        small.done(0)


def weight_grads(xt_top, xt_low, own_t, grad_keys, grad_values, own_gk, own_gv, vec, collective_id):
    width, rows = xt_top.shape
    own_rows = own_gk.shape[0]
    steps = width // BLOCK
    cols = lambda n: pl.BlockSpec((n, BLOCK), lambda i: (0, i))
    r = width // 32
    vr, vw = vec.shape[0] // 32, vec.shape[1]
    outs, vec_sum = pl.pallas_call(
        functools.partial(weight_kernel, steps),
        grid=(steps,),
        in_specs=[
            whole((width, rows)),
            whole((width, rows)),
            whole(own_t.shape),
            cols(rows),
            cols(rows),
            cols(own_rows),
            cols(own_rows),
            ANY,
        ],
        out_specs=[whole((2, r, width)), whole((vr, vw))],
        out_shape=[jax.ShapeDtypeStruct((2, r, width), F32), jax.ShapeDtypeStruct((vr, vw), F32)],
        scratch_shapes=[pltpu.VMEM((2 * steps,) + GRID + (r, BLOCK), F32)]
        + Scatter.scratch(2 * steps, r, BLOCK)
        + [pltpu.VMEM((4, 2, 2, vr, vw), F32), pltpu.SemaphoreType.DMA((1,))]
        + Scatter.scratch(1, vr, vw),
        compiler_params=pltpu.CompilerParams(
            collective_id=collective_id, has_side_effects=True, vmem_limit_bytes=62 * 2**20
        ),
        name="weight_grads",
    )(xt_top, xt_low, own_t, grad_keys, grad_values, own_gk, own_gv, vec.reshape(GRID + (vr, vw)))
    return outs[0], outs[1], vec_sum


def media_back_kernel(plan, steps, *refs):
    feats, embed, gain, grad_keys, grad_values, own_gk, own_gv, key_w, value_w = refs[:9]
    n = plan.arrays
    out, own_out, sums = refs[9 + n : 12 + n]
    kt, kl, vt, vl, stage, sems = refs[12 + 2 * n : 18 + 2 * n]
    step = pl.program_id(0)
    here = Here()
    moved = plan.bind(here, refs[9 : 9 + n], refs[12 + n : 12 + 2 * n], refs[18 + 2 * n :])
    waves = waves_of(moved, moved.count)
    waves[0].insert(0, here.greet)
    pace = Pace(step, steps, 4, 3, waves)

    @pl.when(step == 0)
    def _():
        split_weights((key_w, value_w), ((kt, kl), (vt, vl)), stage, sems, pace)
        own_out[...] = dot3(halves(own_gk[...]), (kt[...], kl[...]), (1, 1)) + dot3(
            halves(own_gv[...]), (vt[...], vl[...]), (1, 1)
        )
        sums[...] = jnp.zeros_like(sums)

    key_pair, value_pair = halves(grad_keys[...]), halves(grad_values[...])
    for i in range(3):
        pace.at(i)
        rows = slice(i * 512, i * 512 + 512)
        out[:, rows] = dot3(key_pair, (kt[rows], kl[rows]), (1, 1)) + dot3(value_pair, (vt[rows], vl[rows]), (1, 1))
    strip = 64

    @pl.loop(0, out.shape[0] // strip)
    def _(i):
        rows = pl.ds(pl.multiple_of(i * strip, strip), strip)
        incoming = out[rows]
        unit, inv_std = unit_of(feats[rows] + embed[...])
        sums[pl.ds(0, 1)] += jnp.sum(incoming * unit, axis=0, keepdims=True)
        sums[pl.ds(1, 1)] += jnp.sum(incoming, axis=0, keepdims=True)
        scaled = incoming * gain[...]
        result = inv_std * (
            scaled
            - jnp.mean(scaled, axis=-1, keepdims=True)
            - unit * jnp.mean(scaled * unit, axis=-1, keepdims=True)
        )
        out[rows] = result
        sums[pl.ds(2 + step, 1)] += jnp.sum(result, axis=0, keepdims=True)

    run_last(step, steps, moved)


def media_backward(feats, embed, gain, grad_keys, grad_values, own_gk, own_gv, key_w, value_w, plan, collective_id):
    rows, width = feats.shape
    own_rows = own_gk.shape[0]
    row_block = pl.BlockSpec((BLOCK, width), lambda i: (i, 0))
    one_block = pl.BlockSpec((BLOCK, width), lambda i: (i, 0), pipeline_mode=pl.Buffered(1))
    steps = rows // BLOCK
    outs = pl.pallas_call(
        functools.partial(media_back_kernel, plan, steps),
        grid=(steps,),
        in_specs=[
            one_block,
            pl.BlockSpec((None, 1, width), lambda i: (i, 0, 0)),
            whole((1, width)),
            row_block,
            row_block,
            whole((own_rows, width)),
            whole((own_rows, width)),
            ANY,
            ANY,
        ]
        + plan.in_specs,
        out_specs=[one_block, whole((own_rows, width)), whole((8, width))] + plan.out_specs,
        out_shape=[
            jax.ShapeDtypeStruct((rows, width), F32),
            jax.ShapeDtypeStruct((own_rows, width), F32),
            jax.ShapeDtypeStruct((8, width), F32),
        ]
        + plan.out_shape,
        scratch_shapes=staging(width) + plan.scratch,
        compiler_params=pltpu.CompilerParams(
            collective_id=collective_id, has_side_effects=True, vmem_limit_bytes=64 * 2**20 - 2**16
        ),
        name="media_backward",
    )(feats, embed, gain, grad_keys, grad_values, own_gk, own_gv, key_w, value_w, *plan.operands)
    return outs[:3], outs[3:]


GELU_A = math.sqrt(2.0 / math.pi)
GELU_B = 0.044715


def feed_kernel(feed, cot, up, down, feed_part, new_part, grad_up_t, grad_down):
    @pl.when(pl.program_id(0) == 0)
    def _():
        grad_up_t[...] = jnp.zeros_like(grad_up_t)
        grad_down[...] = jnp.zeros_like(grad_down)

    hidden = dot(feed[...], up[...])
    grad_act = dot(cot[...], down[...], (1, 1))
    square = hidden * hidden
    bent = jnp.tanh(GELU_A * (hidden + GELU_B * hidden * square))
    activated = 0.5 * hidden * (1.0 + bent)
    slope = 0.5 * (1.0 + bent) + 0.5 * hidden * (1.0 - bent * bent) * (GELU_A * (1.0 + 3.0 * GELU_B * square))
    grad_hidden = grad_act * slope
    feed_part[...] = dot(grad_hidden, up[...], (1, 1))
    new_part[...] = dot(activated, down[...])
    grad_up_t[...] += dot(grad_hidden, feed[...], (0, 0))
    grad_down[...] += dot(activated, cot[...], (0, 0))


def feed_forward(feed, cot, up, down):
    rows, width = feed.shape
    units = up.shape[1]
    row_block = pl.BlockSpec((BLOCK, width), lambda i: (i, 0))
    one_block = pl.BlockSpec((BLOCK, width), lambda i: (i, 0), pipeline_mode=pl.Buffered(1))
    big = jax.ShapeDtypeStruct((rows, width), F32)
    slim = jax.ShapeDtypeStruct((units, width), F32)
    return pl.pallas_call(
        feed_kernel,
        grid=(rows // BLOCK,),
        in_specs=[row_block, row_block, whole((width, units)), whole((units, width))],
        out_specs=[row_block, row_block, whole((units, width)), whole((units, width))],
        out_shape=[big, big, slim, slim],
        compiler_params=pltpu.CompilerParams(vmem_limit_bytes=60 * 2**20),
        name="feed_forward",
    )(feed, cot, up, down)


def mm(left, right):
    return jnp.dot(left, right, precision=HIGH, preferred_element_type=F32)


def mm_tn(left, right):
    return lax.dot_general(left, right, (((0,), (0,)), ((), ())), precision=HIGH, preferred_element_type=F32)


def mm_nt(left, right):
    return lax.dot_general(left, right, (((1,), (1,)), ((), ())), precision=HIGH, preferred_element_type=F32)


def body_fast(
    latents,
    patch_feats,
    image_counts,
    time_index,
    query_proj,
    key_proj,
    value_proj,
    out_proj,
    up_proj,
    down_proj,
    media_gain,
    media_bias,
    latent_gain,
    latent_bias,
    feed_gain,
    feed_bias,
    time_table,
    out_cotangent,
):
    frame = lax.axis_index("frame")
    frames = lax.axis_size("frame")
    seqs, rows, width = latents.shape
    rounds, patches = patch_feats.shape[1], patch_feats.shape[3]
    lat = rows * frames
    head = width // HEADS
    strip = media_gain.shape[0]

    vectors = jnp.concatenate(
        [jnp.stack([media_gain, media_bias, latent_gain, latent_bias, feed_gain, feed_bias]), time_table], axis=0
    )
    packed = jnp.pad(vectors, ((0, 2), (0, 128 - strip)))
    slot_ids = jnp.arange(rounds, dtype=jnp.int32) * frames + frame
    present = slot_ids[None, :] < image_counts[:, None]
    picks = jnp.arange(time_index.shape[1], dtype=jnp.int32)[None, :] == slot_ids[:, None]
    slot_times = jnp.sum(jnp.where(picks[None, :, :], time_index[:, None, :], 0), axis=-1)
    feats = patch_feats.reshape(-1, width)

    (vec_all, keys, values, own_keys, own_values, queries, xt_top, xt_low), gathered, lat_blocks = opening(
        slot_times.reshape(-1), feats, latents, packed, key_proj, value_proj, query_proj, flatten(out_cotangent), out_proj, 0
    )
    key_w, value_w, query_w, cot_all, out_w = gathered
    up_held, keys = lax.optimization_barrier((up_proj, keys))
    up_cols = lax.all_to_all(
        up_held.reshape(strip, 32, -1), ("seq", "frame"), split_axis=1, concat_axis=0, tiled=True
    ).reshape(width, -1)
    mgain, mbias, lgain, lbias, fgain, fbias = (vec_all[i] for i in range(6))
    table = vec_all[6:14]
    queries = queries.reshape(seqs, lat, width)
    latent_norm, latent_unit, latent_std = norm_forward(lat_blocks.reshape(seqs, lat, width), lgain, lbias)
    own_rows = lambda v: lax.dynamic_slice_in_dim(v, frame * rows, rows, 1)
    own_norm, own_unit, own_std = own_rows(latent_norm), own_rows(latent_unit), own_rows(latent_std)
    one_hot = slot_times[:, :, None] == jnp.arange(time_table.shape[0], dtype=jnp.int32)
    slot_embed = jnp.sum(jnp.where(one_hot[..., None], table, 0.0), axis=2)
    embed = slot_embed.reshape(-1, 1, width)
    own_flat = flatten(own_norm)
    present = present.astype(jnp.int32)

    partial, row_top, row_sum = attend(present, queries, keys, values, own_keys, own_values)
    stats = jnp.concatenate([row_top.reshape(seqs, HEADS, lat), row_sum.reshape(seqs, HEADS, lat)], axis=1)
    stats = jnp.pad(stats.transpose(0, 2, 1), ((0, 0), (0, 0), (0, 128 - 2 * HEADS)))
    part_all, stat_all = group_swap(
        [partial.reshape(seqs, frames, rows, width), stats.reshape(seqs, frames, rows, 128)], 2
    )
    tops, sums = stat_all[..., :HEADS], stat_all[..., HEADS : 2 * HEADS]
    top = jnp.max(tops, axis=1)
    ratio = jnp.exp(tops - top[:, None])
    row_total = jnp.sum(sums * ratio, axis=1)
    weight = ratio / row_total[:, None]
    attended = jnp.sum(part_all.reshape(seqs, frames, rows, HEADS, head) * weight[..., None], axis=1)
    log_total = top + jnp.log(row_total)
    attended_flat = attended.reshape(seqs, rows, width)
    middle = latents + mm(flatten(attended_flat), out_w).reshape(seqs, rows, width)

    feed_norm, feed_unit, feed_std = norm_forward(middle, fgain, fbias)
    (feed_all,) = gather_all([flatten(feed_norm)], 3)
    feed_part, new_part, grad_up_t, grad_down = feed_forward(feed_all, cot_all, up_cols, down_proj)
    (grad_feed_norm,) = scatter_all([feed_part], 4)
    grad_mid_norm, grad_fgain, grad_fbias = norm_backward(
        grad_feed_norm.reshape(seqs, rows, width), feed_unit, feed_std, fgain
    )
    grad_middle = out_cotangent + grad_mid_norm
    grad_out_w = mm_tn(flatten(attended_flat), flatten(grad_middle))
    grad_own = mm_nt(flatten(grad_middle), out_w).reshape(seqs, rows, HEADS, head)
    delta = jnp.sum(grad_own * attended, axis=-1)
    back_stats = jnp.pad(jnp.concatenate([log_total, delta], axis=-1), ((0, 0), (0, 0), (0, 128 - 2 * HEADS)))
    grad_blocks, back_blocks = group_gather([grad_own.reshape(seqs, rows, width), back_stats], 5)
    back_all = back_blocks.reshape(seqs, lat, 128).transpose(0, 2, 1)
    logs_all, delta_all = (back_all[:, i * HEADS : (i + 1) * HEADS].reshape(seqs, 8, 128) for i in range(2))

    (query_part, grad_keys, grad_values, own_gk, own_gv), (new_rows,) = attend_back(
        present,
        queries,
        grad_blocks.reshape(seqs, lat, width),
        logs_all,
        delta_all,
        keys,
        values,
        own_keys,
        own_values,
        Summed([new_part]),
        10,
    )
    new_latents = middle + new_rows.reshape(seqs, rows, width)
    grad_up_t, query_part = lax.optimization_barrier((grad_up_t, query_part))
    grad_up = lax.all_to_all(
        grad_up_t.reshape(-1, 32, strip).transpose(1, 2, 0), ("seq", "frame"), split_axis=0, concat_axis=2, tiled=True
    ).reshape(strip, -1)
    (query_blocks,) = group_swap([query_part.reshape(seqs, frames, rows, width)], 6)
    grad_queries = flatten(jnp.sum(query_blocks, axis=1))

    grad_query_w = mm_tn(own_flat, grad_queries)
    grad_up, grad_query_w = lax.optimization_barrier((grad_up, grad_query_w))
    (patch_grads, own_back, media_sums), (sum_query, sum_out) = media_backward(
        feats,
        embed,
        mgain[None],
        grad_keys,
        grad_values,
        own_gk,
        own_gv,
        key_w,
        value_w,
        Summed([grad_query_w, grad_out_w]),
        7,
    )
    grad_own_norm = (mm_nt(grad_queries, query_w) + own_back).reshape(seqs, rows, width)
    grad_lat_in, grad_lgain, grad_lbias = norm_backward(grad_own_norm, own_unit, own_std, lgain)
    latent_grads = grad_middle + grad_lat_in
    grad_mgain, grad_mbias = media_sums[0], media_sums[1]
    slot_sums = media_sums[2:].reshape(seqs, rounds, width)
    grad_table = jnp.sum(jnp.where(one_hot[..., None], slot_sums[:, :, None, :], 0.0), axis=(0, 1))
    vec_grads = jnp.concatenate(
        [jnp.stack([grad_mgain, grad_mbias, grad_lgain, grad_lbias, grad_fgain, grad_fbias]), grad_table], axis=0
    )
    vec_blocks = jnp.pad(vec_grads.reshape(14, 32, strip).transpose(1, 0, 2), ((0, 0), (0, 2), (0, 128 - strip)))
    top, low = halves(own_flat)
    own_t = jnp.concatenate([top, top, low], axis=0).T
    sum_key, sum_value, sum_vec = weight_grads(
        xt_top, xt_low, own_t, grad_keys, grad_values, own_gk, own_gv, vec_blocks.reshape(-1, 128), 8
    )
    vec = sum_vec[:14, :strip]
    return (
        new_latents,
        latent_grads,
        patch_grads.reshape(patch_feats.shape),
        sum_query,
        sum_key,
        sum_value,
        sum_out,
        grad_up,
        grad_down,
        vec[0],
        vec[1],
        vec[2],
        vec[3],
        vec[4],
        vec[5],
        vec[6:],
    )


def solution(mesh):
    fast = dict(mesh.shape) == {"seq": 8, "frame": 4}
    return jax.shard_map(
        body_fast if fast else body_general,
        mesh=mesh,
        in_specs=(
            P("seq", "frame", None),
            P("seq", None, "frame", None, None),
            P("seq"),
            P("seq", None),
            P(("seq", "frame"), None),
            P(("seq", "frame"), None),
            P(("seq", "frame"), None),
            P(("seq", "frame"), None),
            P(("seq", "frame"), None),
            P(("seq", "frame"), None),
            P(("seq", "frame")),
            P(("seq", "frame")),
            P(("seq", "frame")),
            P(("seq", "frame")),
            P(("seq", "frame")),
            P(("seq", "frame")),
            P(None, ("seq", "frame")),
            P("seq", "frame", None),
        ),
        out_specs=(
            P("seq", "frame", None),
            P("seq", "frame", None),
            P("seq", None, "frame", None, None),
            P(("seq", "frame"), None),
            P(("seq", "frame"), None),
            P(("seq", "frame"), None),
            P(("seq", "frame"), None),
            P(("seq", "frame"), None),
            P(("seq", "frame"), None),
            P(("seq", "frame")),
            P(("seq", "frame")),
            P(("seq", "frame")),
            P(("seq", "frame")),
            P(("seq", "frame")),
            P(("seq", "frame")),
            P(None, ("seq", "frame")),
        ),
        check_vma=False,
    )
```

profile of v0, /device:TPU:0, one launch (start us, length us, event | category | flops | bytes accessed | tf_op | source)
XLA Modules:
  0.0 859.1 jit_solution(17340153268739001103)
XLA Ops:
  4.3 231.4 %opening.1 = (f32[16,1536]{1,0:T(8,128)}, f32[1536,1536]{1,0:T(8,128)}, f32[1536,1536]{1,0:T(8,128)}, f32[48,1536]{1,0:T(8,128)}, f32[48,1536]{1,0:T(8,128)}, /*...) custom-call(s32[6]{0:T(128)} %reshape.302.refs_0_, ...), custom_call_target="tpu_custom_call" | custom-call | tf_op jit(solution)/shard_map/opening/pallas_call | solution.py:1049
  236.4 2.1 copy.77
  238.5 4.0 all-to-all-start
  243.2 27.2 %attend.1 = (f32[3,64,1536]{2,1,0:T(8,128)}, f32[3,8,128]{2,1,0:T(8,128)}, f32[3,8,128]{2,1,0:T(8,128)}) custom-call(s32[3,2]{1,0:T(4,128)} %compare_convert_fusion.present.refs_0_, f32[3,64,1536]{2,1,0:T(8,128)} %bitcast.129, f32[1536,1536]{1,0:T(8,128)} %get-tuple-element.62.keys.refs_5_, f32[1536,1536]{1,0:T(8,128)} %get-tuple-element.63.values.refs_6_, ...), custom_call_target="tpu_custom_call" | custom-call | tf_op jit(solution)/shard_map/attend/pallas_call | solution.py:1163
  272.9 18.1 %group_swap.2 = (f32[3,4,16,1536]{3,2,1,0:T(8,128)}, f32[3,4,16,128]{3,2,1,0:T(8,128)}) custom-call(f32[3,4,16,1536]{3,2,1,0:T(8,128)} %bitcast.142, f32[3,4,16,128]{3,2,1,0:T(8,128)} %bitcast.144), custom_call_target="tpu_custom_call" | custom-call | tf_op jit(solution)/shard_map/group_swap/pallas_call | solution.py:874
  294.4 1.8 mul.147
  298.0 6.8 fusion.7
  307.6 47.9 %gather_all.1 = f32[4,2,2,2,48,1536]{5,4,3,2,1,0:T(8,128)} custom-call(f32[48,1536]{1,0:T(8,128)} %bitcast.138), custom_call_target="tpu_custom_call" | custom-call | tf_op jit(solution)/shard_map/gather_all/pallas_call | solution.py:718
  357.1 27.3 %feed_forward.1 = (f32[1536,1536]{1,0:T(8,128)}, f32[1536,1536]{1,0:T(8,128)}, f32[192,1536]{1,0:T(8,128)}, f32[192,1536]{1,0:T(8,128)}) custom-call(f32[1536,1536]{1,0:T(8,128)} %bitcast.114, f32[1536,1536]{1,0:T(8,128)} %bitcast.120, f32[1536,192]{1,0:T(8,128)} %bitcast.20.up, f32[192,1536]{1,0:T(8,128)} %down.1), custom_call_target="tpu_custom_call" | custom-call | tf_op jit(solution)/shard_map/feed_forward/pallas_call | solution.py:1446
  384.4 58.9 %scatter_all.1 = f32[48,1536]{1,0:T(8,128)} custom-call(f32[4,2,2,2,48,1536]{5,4,3,2,1,0:T(8,128)} %bitcast.117), custom_call_target="tpu_custom_call" | custom-call | tf_op jit(solution)/shard_map/scatter_all/pallas_call | solution.py:782
  445.6 1.9 multiply_add_fusion.1
  447.6 8.1 fusion.8
  456.7 11.6 %group_gather.1 = (f32[3,4,16,1536]{3,2,1,0:T(8,128)}, f32[3,4,16,128]{3,2,1,0:T(8,128)}) custom-call(f32[3,16,1536]{2,1,0:T(8,128)} %bitcast.135, f32[3,16,128]{2,1,0:T(8,128)} %select_maximum_fusion.refs_1_), custom_call_target="tpu_custom_call" | custom-call | tf_op jit(solution)/shard_map/group_gather/pallas_call | solution.py:836
  470.7 60.3 %attend_back.1 = (f32[3,64,1536]{2,1,0:T(8,128)}, f32[1536,1536]{1,0:T(8,128)}, f32[1536,1536]{1,0:T(8,128)}, f32[48,1536]{1,0:T(8,128)}, f32[48,1536]{1,0:T(8,128)}, /*index=5*/f32[48,1536]{1,0:T(8,128)}) custom-call(s32[3,2]{1,0:T(4,128)} %compare_convert_fusion.present.refs_0_, f32[3,64,1536]{2,1,0:T(8,128)} %bitcast.130, f32[3,64,1536]{2,1,0:T(8,128)} %bitcast.137, ...), custom_call_target="tpu_custom_call" | custom-call | tf_op jit(solution)/shard_map/attend_back/pallas_call | solution.py:1214
  532.7 5.1 all-to-all-start.1
  539.2 28.5 %group_swap.3 = f32[3,4,16,1536]{3,2,1,0:T(8,128)} custom-call(f32[3,4,16,1536]{3,2,1,0:T(8,128)} %bitcast.141), custom_call_target="tpu_custom_call" | custom-call | tf_op jit(solution)/shard_map/group_swap/pallas_call | solution.py:874
  567.7 2.1 reduce_sum.184
  577.1 6.3 convolution_bitcast_fusion
  583.4 6.2 fusion.9.refs_10_
  592.1 128.6 %media_backward.1 = (f32[1536,1536]{1,0:T(8,128)}, f32[48,1536]{1,0:T(8,128)}, f32[8,1536]{1,0:T(8,128)}, f32[48,1536]{1,0:T(8,128)}, f32[48,1536]{1,0:T(8,128)}) custom-call(f32[1536,1536]{1,0:T(8,128)} %bitcast.113, f32[6,1,1536]{2,1,0:T(1,128)} %reshape.330.refs_1_, f32[1,1536]{1,0:T(1,128)} %get-tuple-element.202.refs_2_, ...), custom_call_target="tpu_custom_call" | custom-call | tf_op jit(solution)/shard_map/media_backward/pallas_call | solution.py:1385
  722.3 8.3 fusion.5
  732.0 110.6 %weight_grads.1 = (f32[2,48,1536]{2,1,0:T(8,128)}, f32[16,128]{1,0:T(8,128)}) custom-call(bf16[1536,1536]{1,0:T(8,128)(2,1)} %get-tuple-element.96.xt_top, bf16[1536,1536]{1,0:T(8,128)(2,1)} %get-tuple-element.97.xt_low, bf16[1536,144]{1,0:T(8,128)(2,1)} %maximum_bitcast_fusion.own_t, f32[1536,1536]{1,0:T(8,128)} %get-tuple-element.85.refs_3_.grad_keys, ...), custom_call_target="tpu_custom_call" | custom-call | tf_op jit(solution)/shard_map/weight_grads/pallas_call | solution.py:1306
  845.4 1.9 slice_bitcast_fusion
  848.4 9.1 %copy.98 = f32[3,2,1,256,1536]{4,3,2,1,0:T(8,128)} copy(f32[3,2,1,256,1536]{4,3,2,1,0:T(8,128)} %bitcast.116) | data formatting | bytes 18874368
  (142 shorter events, 43.9 us)
Async XLA Ops:
  4.3 231.4 %copy-start.12 = (f32[48,6144]{1,0:T(8,128)S(1)}, f32[48,6144]{1,0:T(8,128)}, u32[]{:S(2)}) copy-start(f32[48,6144]{1,0:T(8,128)} %param.26) | copy-start | bytes 3538948
  238.5 4.0 copy-start.25
  238.5 118.6 %all-to-all-start = ((f32[48,32,192]{2,0,1:T(8,128)}), f32[48,32,192]{2,0,1:T(8,128)}, u32[]{:S(2)}, u32[]{:S(2)}) async-start(f32[48,32,192]{2,0,1:T(8,128)} %copy.77), calls=%async_computation | async-start | bytes 3145728 | tf_op jit(solution)/shard_map/all_to_all | solution.py:1512
  294.4 1.8 copy-start
  298.0 8.0 copy-start.21
  306.8 138.8 %copy-start.17 = (f32[1536]{0:T(1024)}, f32[1536]{0:T(1024)S(1)}, u32[]{:S(2)}) copy-start(f32[1536]{0:T(1024)S(1)} %get-tuple-element.190) | copy-start | bytes 18436
  355.8 181.9 %copy-start.22 = (pred[3,2,8]{2,1,0:T(4,128)(4,1)}, pred[3,2,8]{2,1,0:T(4,128)(4,1)S(1)}, u32[]{:S(2)}) copy-start(pred[3,2,8]{2,1,0:T(4,128)(4,1)S(1)} %iota_compare_fusion.1) | copy-start | bytes 148
  384.4 61.2 %copy-start.10 = (f32[3,16,1536]{2,1,0:T(8,128)S(1)}, f32[3,16,1536]{2,1,0:T(8,128)}, u32[]{:S(2)}) copy-start(f32[3,16,1536]{2,1,0:T(8,128)} %param.35) | copy-start | bytes 884740
  447.6 135.8 %copy-start.1 = (f32[3,16,1536]{2,1,0:T(8,128)}, f32[3,16,1536]{2,1,0:T(8,128)S(1)}, u32[]{:S(2)}) copy-start(f32[3,16,1536]{2,1,0:T(8,128)S(1)} %get-tuple-element.212) | copy-start | bytes 884740
  447.6 8.3 copy-start.9
  470.7 60.3 %copy-start.13 = (f32[192,1536]{1,0:T(8,128)S(1)}, f32[192,1536]{1,0:T(8,128)}, u32[]{:S(2)}) copy-start(f32[192,1536]{1,0:T(8,128)} %get-tuple-element.91) | copy-start | bytes 3538948
  532.7 56.8 %all-to-all-start.1 = ((f32[32,48,192]{2,1,0:T(8,128)}), f32[32,48,192]{2,1,0:T(8,128)S(1)}, u32[]{:S(2)}, u32[]{:S(2)}) async-start(f32[32,48,192]{2,1,0:T(8,128)} %bitcast.37), calls=%async_computation.1 | async-start | bytes 3145728 | tf_op jit(solution)/shard_map/all_to_all | solution.py:1574
  539.2 31.9 %copy-start.7 = (f32[3,16,1536]{2,1,0:T(8,128)S(1)}, f32[3,16,1536]{2,1,0:T(8,128)}, u32[]{:S(2)}) copy-start(f32[3,16,1536]{2,1,0:T(8,128)} %get-tuple-element.194) | copy-start | bytes 884740
  574.3 2.8 copy-start.8
  574.3 2.8 copy-start.11
  722.3 8.6 copy-start.23
  722.3 8.8 %copy-start.19 = (f32[1,32,48]{2,1,0:T(8,128)S(1)}, f32[1,32,48]{2,1,0:T(8,128)}, u32[]{:S(2)}) copy-start(f32[1,32,48]{2,1,0:T(8,128)} %concatenate.36) | copy-start | bytes 18436
  722.3 8.8 %copy-start.20 = (f32[1,32,48]{2,1,0:T(8,128)S(1)}, f32[1,32,48]{2,1,0:T(8,128)}, u32[]{:S(2)}) copy-start(f32[1,32,48]{2,1,0:T(8,128)} %concatenate.37) | copy-start | bytes 18436
  732.0 115.3 %copy-start.3 = (f32[3,16,1536]{2,1,0:T(8,128)S(1)}, f32[3,16,1536]{2,1,0:T(8,128)}, u32[]{:S(2)}) copy-start(f32[3,16,1536]{2,1,0:T(8,128)} %get-tuple-element.195) | copy-start | bytes 884740
  732.0 115.3 %copy-start.18 = (f32[1536]{0:T(1024)S(1)}, f32[1536]{0:T(1024)}, u32[]{:S(2)}) copy-start(f32[1536]{0:T(1024)} %copy-done.17) | copy-start | bytes 18436
  842.6 4.9 copy-start.2
  842.6 4.9 copy-start.24
  848.4 9.1 %copy-start.16 = (f32[48,1536]{1,0:T(8,128)S(1)}, f32[48,1536]{1,0:T(8,128)}, u32[]{:S(2)}) copy-start(f32[48,1536]{1,0:T(8,128)} %get-tuple-element.232) | copy-start | bytes 884740
  848.4 9.8 %copy-start.15 = (f32[48,1536]{1,0:T(8,128)S(1)}, f32[48,1536]{1,0:T(8,128)}, u32[]{:S(2)}) copy-start(f32[48,1536]{1,0:T(8,128)} %get-tuple-element.235) | copy-start | bytes 884740
  (4 other events, 5.3 us)
where the time goes:
time: 868 us; the launch traced here: 859 us
  Pallas kernels  750 us (86%)
  local copies, waits for them, and re-layouts  42.4 us (5%)
  matrix products  35.6 us (4%)
  other arithmetic  20.3 us (2%)
  starting transfers between devices  9.08 us (1%)
    pallas_call x1, Pallas kernels, opening(): pl.pallas_call(functools.partial(opening_kernel, cuts), grid=(slots + 2 *...  231 us
    pallas_call x1, Pallas kernels, media_backward(): pl.pallas_call(functools.partial(media_back_kernel, plan, steps), grid=(s...  129 us
    pallas_call x1, Pallas kernels, weight_grads(): pl.pallas_call(functools.partial(weight_kernel, steps), grid=(steps,), in...  111 us
    pallas_call x1, Pallas kernels, attend_back(): pl.pallas_call(functools.partial(attend_back_kernel, 1.0 / math.sqrt(head...  60.3 us
    pallas_call x1, Pallas kernels, scatter_all(): pl.pallas_call(functools.partial(scatter_kernel, plan), out_shape=plan.ou...  58.9 us
    pallas_call x1, Pallas kernels, gather_all(): pl.pallas_call(functools.partial(gather_kernel, count, cuts), out_shape=f...  47.9 us
    pallas_call x2, Pallas kernels, group_swap(): pl.pallas_call(functools.partial(group_swap_kernel, count), out_shape=[ja...  46.5 us
    pallas_call x1, Pallas kernels, feed_forward(): pl.pallas_call(feed_kernel, grid=(rows // BLOCK,), in_specs=[row_block, r...  27.3 us
  transfers between devices with their start and end apart: 2, of which 0 were waited for; matrix products, arithmetic and copies ran while one was open for 5% of the time, Pallas kernels for 14%

commit v1 on v0

--- a/solution.py
+++ b/solution.py
@@ -880,6 +880,58 @@
         compiler_params=pltpu.CompilerParams(collective_id=collective_id, has_side_effects=True),
         name="group_swap",
     )(*shards)
+
+
+def group_sum_kernel(parts, out, tot, got, last, loc, ss, rs):
+    here = Here()
+    greet([here.at_x, here.at_c])
+    load = pltpu.make_async_copy(parts.at[:, :, here.c], tot, loc.at[0])
+    load.start()
+    side = remote(parts.at[:, :, here.oc], got, ss.at[0], rs.at[0], here.at_c)
+    side.start()
+    load.wait()
+    side.wait_recv()
+    tot[...] += got[...]
+    over = remote(tot.at[:, here.ox], last, ss.at[1], rs.at[1], here.at_x)
+    over.start()
+    over.wait_recv()
+    out[...] = tot[:, here.x] + last[...]
+    side.wait_send()
+    over.wait_send()
+
+
+def group_sum(parts, collective_id):
+    s, lat, w = parts.shape
+    r = lat // 4
+    dma = pltpu.SemaphoreType.DMA
+    return pl.pallas_call(
+        group_sum_kernel,
+        out_shape=jax.ShapeDtypeStruct((s, r, w), F32),
+        in_specs=[ANY],
+        out_specs=pl.BlockSpec(memory_space=pltpu.VMEM),
+        scratch_shapes=[
+            pltpu.VMEM((s, 2, r, w), F32),
+            pltpu.VMEM((s, 2, r, w), F32),
+            pltpu.VMEM((s, r, w), F32),
+            dma((1,)),
+            dma((2,)),
+            dma((2,)),
+        ],
+        compiler_params=pltpu.CompilerParams(collective_id=collective_id, has_side_effects=True),
+        name="group_sum",
+    )(parts.reshape(s, 2, 2, r, w))
+
+
+def stacked(values, axis, order):
+    top = lax.reduce_precision(values, 8, 7)
+    terms = (top.astype(jnp.bfloat16), (values - top).astype(jnp.bfloat16))
+    return jnp.concatenate([terms[i] for i in order], axis=axis)
+
+
+def thin_product(left, right):
+    return lax.dot_general(
+        stacked(left, 0, (0, 0, 1)), stacked(right, 0, (0, 1, 0)), (((0,), (0,)), ((), ())), preferred_element_type=F32
+    )
 
 
 BF16 = jnp.bfloat16
@@ -1417,39 +1469,89 @@
 GELU_B = 0.044715
 
 
-def feed_kernel(feed, cot, up, down, feed_part, new_part, grad_up_t, grad_down):
-    @pl.when(pl.program_id(0) == 0)
+def feed_kernel(blocks, *refs):
+    feed, cot, up, down, new_part, grad_up_t, grad_down, out, act, back, mats = refs[:11]
+    step = pl.program_id(0)
+    here = Here()
+    pieces, cut = mats.shape[0], mats.shape[-1]
+    sums = Scatter(
+        here,
+        pieces,
+        lambda p: mats.at[p, :, :, :, here.c],
+        lambda p: mats.at[p, :, :, :, here.oc],
+        None,
+        lambda p: out.at[:, p * cut : (p + 1) * cut],
+        refs[11:],
+    )
+    waves = waves_of(sums, pieces)
+    block = step - blocks * (step >= blocks).astype(jnp.int32)
+    rows = pl.ds(pl.multiple_of(block * BLOCK, BLOCK), BLOCK)
+    pl.when(step == 0)(here.greet)
+
+    @pl.when(step < blocks)
     def _():
+        hidden = dot(feed[...], up[...])
+        grad_act = dot(cot[...], down[...], (1, 1))
+        square = hidden * hidden
+        bent = jnp.tanh(GELU_A * (hidden + GELU_B * hidden * square))
+        slope = 0.5 * (1.0 + bent) + 0.5 * hidden * (1.0 - bent * bent) * (GELU_A * (1.0 + 3.0 * GELU_B * square))
+        act[rows] = 0.5 * hidden * (1.0 + bent)
+        back[rows] = grad_act * slope
+
+    @pl.when(step == blocks)
+    def _():
+        for p in range(pieces):
+
+            @pl.loop(0, 4)
+            def _(zi):
+                plane = pl.ds(pl.multiple_of(zi * 384, 384), 384)
+                made = dot(back[plane], up[p * cut : (p + 1) * cut], (1, 1))
+                mats[p, zi] = made.reshape((2, 2, 2, 48, cut))
+
+            sums.start(p)
         grad_up_t[...] = jnp.zeros_like(grad_up_t)
         grad_down[...] = jnp.zeros_like(grad_down)
 
-    hidden = dot(feed[...], up[...])
-    grad_act = dot(cot[...], down[...], (1, 1))
-    square = hidden * hidden
-    bent = jnp.tanh(GELU_A * (hidden + GELU_B * hidden * square))
-    activated = 0.5 * hidden * (1.0 + bent)
-    slope = 0.5 * (1.0 + bent) + 0.5 * hidden * (1.0 - bent * bent) * (GELU_A * (1.0 + 3.0 * GELU_B * square))
-    grad_hidden = grad_act * slope
-    feed_part[...] = dot(grad_hidden, up[...], (1, 1))
-    new_part[...] = dot(activated, down[...])
-    grad_up_t[...] += dot(grad_hidden, feed[...], (0, 0))
-    grad_down[...] += dot(activated, cot[...], (0, 0))
-
-
-def feed_forward(feed, cot, up, down):
+    for i in range(blocks):
+
+        @pl.when(step == blocks + i)
+        def _():
+            for wave in waves[1 + 2 * i : 3 + 2 * i]:
+                run(wave)
+
+    @pl.when(step >= blocks)
+    def _():
+        new_part[...] = dot(act[rows], down[...])
+        grad_up_t[...] += dot(back[rows], feed[...], (0, 0))
+        grad_down[...] += dot(act[rows], cot[...], (0, 0))
+
+    @pl.when(step == 2 * blocks - 1)
+    def _():
+        for wave in waves[1 + 2 * blocks :]:
+            run(wave)
+        finish_all(sums)
+
+
+def feed_forward(feed, cot, up, down, collective_id):
     rows, width = feed.shape
-    units = up.shape[1]
-    row_block = pl.BlockSpec((BLOCK, width), lambda i: (i, 0))
-    one_block = pl.BlockSpec((BLOCK, width), lambda i: (i, 0), pipeline_mode=pl.Buffered(1))
+    units, r, cut = up.shape[1], width // 32, 256
+    blocks = rows // BLOCK
     big = jax.ShapeDtypeStruct((rows, width), F32)
     slim = jax.ShapeDtypeStruct((units, width), F32)
+    row_block = pl.BlockSpec((BLOCK, width), lambda i: (i % blocks, 0))
+    late_block = pl.BlockSpec((BLOCK, width), lambda i: (jnp.maximum(i - blocks, 0), 0))
     return pl.pallas_call(
-        feed_kernel,
-        grid=(rows // BLOCK,),
+        functools.partial(feed_kernel, blocks),
+        grid=(2 * blocks,),
         in_specs=[row_block, row_block, whole((width, units)), whole((units, width))],
-        out_specs=[row_block, row_block, whole((units, width)), whole((units, width))],
-        out_shape=[big, big, slim, slim],
-        compiler_params=pltpu.CompilerParams(vmem_limit_bytes=60 * 2**20),
+        out_specs=[late_block, whole((units, width)), whole((units, width)), whole((r, width))],
+        out_shape=[big, slim, slim, jax.ShapeDtypeStruct((r, width), F32)],
+        scratch_shapes=[pltpu.VMEM((rows, units), F32)] * 2
+        + [pltpu.VMEM((width // cut,) + GRID + (r, cut), F32)]
+        + Scatter.scratch(width // cut, r, cut),
+        compiler_params=pltpu.CompilerParams(
+            collective_id=collective_id, has_side_effects=True, vmem_limit_bytes=60 * 2**20
+        ),
         name="feed_forward",
     )(feed, cot, up, down)
 
@@ -1542,13 +1644,15 @@
 
     feed_norm, feed_unit, feed_std = norm_forward(middle, fgain, fbias)
     (feed_all,) = gather_all([flatten(feed_norm)], 3)
-    feed_part, new_part, grad_up_t, grad_down = feed_forward(feed_all, cot_all, up_cols, down_proj)
-    (grad_feed_norm,) = scatter_all([feed_part], 4)
+    new_part, grad_up_t, grad_down, grad_feed_norm = feed_forward(feed_all, cot_all, up_cols, down_proj, 4)
+    grad_up = lax.all_to_all(
+        grad_up_t.reshape(-1, 32, strip).transpose(1, 2, 0), ("seq", "frame"), split_axis=0, concat_axis=2, tiled=True
+    ).reshape(strip, -1)
     grad_mid_norm, grad_fgain, grad_fbias = norm_backward(
         grad_feed_norm.reshape(seqs, rows, width), feed_unit, feed_std, fgain
     )
     grad_middle = out_cotangent + grad_mid_norm
-    grad_out_w = mm_tn(flatten(attended_flat), flatten(grad_middle))
+    grad_out_w = thin_product(flatten(attended_flat), flatten(grad_middle))
     grad_own = mm_nt(flatten(grad_middle), out_w).reshape(seqs, rows, HEADS, head)
     delta = jnp.sum(grad_own * attended, axis=-1)
     back_stats = jnp.pad(jnp.concatenate([log_total, delta], axis=-1), ((0, 0), (0, 0), (0, 128 - 2 * HEADS)))
@@ -1570,15 +1674,9 @@
         10,
     )
     new_latents = middle + new_rows.reshape(seqs, rows, width)
-    grad_up_t, query_part = lax.optimization_barrier((grad_up_t, query_part))
-    grad_up = lax.all_to_all(
-        grad_up_t.reshape(-1, 32, strip).transpose(1, 2, 0), ("seq", "frame"), split_axis=0, concat_axis=2, tiled=True
-    ).reshape(strip, -1)
-    (query_blocks,) = group_swap([query_part.reshape(seqs, frames, rows, width)], 6)
-    grad_queries = flatten(jnp.sum(query_blocks, axis=1))
-
-    grad_query_w = mm_tn(own_flat, grad_queries)
-    grad_up, grad_query_w = lax.optimization_barrier((grad_up, grad_query_w))
+    grad_queries = flatten(group_sum(query_part, 6))
+
+    grad_query_w = thin_product(own_flat, grad_queries)
     (patch_grads, own_back, media_sums), (sum_query, sum_out) = media_backward(
         feats,
         embed,
@@ -1602,8 +1700,7 @@
         [jnp.stack([grad_mgain, grad_mbias, grad_lgain, grad_lbias, grad_fgain, grad_fbias]), grad_table], axis=0
     )
     vec_blocks = jnp.pad(vec_grads.reshape(14, 32, strip).transpose(1, 0, 2), ((0, 0), (0, 2), (0, 128 - strip)))
-    top, low = halves(own_flat)
-    own_t = jnp.concatenate([top, top, low], axis=0).T
+    own_t = stacked(own_flat, 0, (0, 0, 1)).T
     sum_key, sum_value, sum_vec = weight_grads(
         xt_top, xt_low, own_t, grad_keys, grad_values, own_gk, own_gv, vec_blocks.reshape(-1, 128), 8
     )

time: 868 us -> 850 us (0.979)
  Pallas kernels: 750 us -> 733 us
    pallas_call x2 -> x1, Pallas kernels: 46.5 us -> 17.1 us  [group_swap(): pl.pallas_call(functools.partial(group_swap_kernel, count), out_shape=[ja...]
    pallas_call x2, Pallas kernels: 86.2 us -> 95.8 us  [the longest x1 83.3 us: feed_forward(): pl.pallas_call(functools.partial(feed_kernel, blocks), grid=(2 * blocks,)...]
  transfers between devices with their start and end apart: 2 -> 2, of which waited for: 0 -> 0; matrix products, arithmetic and copies ran while one was open for 5% -> 4% of each run, Pallas kernels for 14% -> 25%
where the time goes in v1:
time: 850 us; the launch traced here: 841 us
  Pallas kernels  733 us (86%)
  local copies, waits for them, and re-layouts  45.3 us (5%)
  matrix products  34.1 us (4%)
  other arithmetic  18.8 us (2%)
    pallas_call x1, Pallas kernels, opening(): pl.pallas_call(functools.partial(opening_kernel, cuts), grid=(slots + 2 *...  231 us
    pallas_call x1, Pallas kernels, media_backward(): pl.pallas_call(functools.partial(media_back_kernel, plan, steps), grid=(s...  127 us
    pallas_call x1, Pallas kernels, weight_grads(): pl.pallas_call(functools.partial(weight_kernel, steps), grid=(steps,), in...  115 us
    pallas_call x1, Pallas kernels, feed_forward(): pl.pallas_call(functools.partial(feed_kernel, blocks), grid=(2 * blocks,)...  83.3 us
    pallas_call x1, Pallas kernels, attend_back(): pl.pallas_call(functools.partial(attend_back_kernel, 1.0 / math.sqrt(head...  60.4 us
    pallas_call x1, Pallas kernels, gather_all(): pl.pallas_call(functools.partial(gather_kernel, count, cuts), out_shape=f...  48 us
    pallas_call x1, Pallas kernels, attend(): pl.pallas_call(functools.partial(attend_kernel, 1.0 / math.sqrt(head), he...  27.2 us
    pallas_call x1, Pallas kernels, group_swap(): pl.pallas_call(functools.partial(group_swap_kernel, count), out_shape=[ja...  17.1 us
  transfers between devices with their start and end apart: 2, of which 0 were waited for; matrix products, arithmetic and copies ran while one was open for 4% of the time, Pallas kernels for 25%

profile of v1, /device:TPU:0, one launch (start us, length us, event | category | flops | bytes accessed | tf_op | source)
XLA Modules:
  0.0 841.3 jit_solution(3458707463393446998)
XLA Ops:
  4.3 231.5 %opening.1 = (f32[16,1536]{1,0:T(8,128)}, f32[1536,1536]{1,0:T(8,128)}, f32[1536,1536]{1,0:T(8,128)}, f32[48,1536]{1,0:T(8,128)}, f32[48,1536]{1,0:T(8,128)}, /*...) custom-call(s32[6]{0:T(128)} %reshape.300.refs_0_, ...), custom_call_target="tpu_custom_call" | custom-call | tf_op jit(solution)/shard_map/opening/pallas_call | solution.py:1101
  236.5 2.1 copy.73
  238.6 3.8 all-to-all-start
  246.1 27.2 %attend.1 = (f32[3,64,1536]{2,1,0:T(8,128)}, f32[3,8,128]{2,1,0:T(8,128)}, f32[3,8,128]{2,1,0:T(8,128)}) custom-call(s32[3,2]{1,0:T(4,128)} %compare_convert_fusion.present.refs_0_, f32[3,64,1536]{2,1,0:T(8,128)} %bitcast.119, f32[1536,1536]{1,0:T(8,128)} %get-tuple-element.58.keys.refs_5_, f32[1536,1536]{1,0:T(8,128)} %get-tuple-element.59.values.refs_6_, ...), custom_call_target="tpu_custom_call" | custom-call | tf_op jit(solution)/shard_map/attend/pallas_call | solution.py:1215
  275.8 17.1 %group_swap.1 = (f32[3,4,16,1536]{3,2,1,0:T(8,128)}, f32[3,4,16,128]{3,2,1,0:T(8,128)}) custom-call(f32[3,4,16,1536]{3,2,1,0:T(8,128)} %bitcast.132, f32[3,4,16,128]{3,2,1,0:T(8,128)} %bitcast.135), custom_call_target="tpu_custom_call" | custom-call | tf_op jit(solution)/shard_map/group_swap/pallas_call | solution.py:874
  296.4 1.8 mul.147
  298.1 1.8 multiply_reduce_fusion.1
  300.9 6.8 fusion.31
  309.2 48.0 %gather_all.1 = f32[4,2,2,2,48,1536]{5,4,3,2,1,0:T(8,128)} custom-call(f32[48,1536]{1,0:T(8,128)} %bitcast.130), custom_call_target="tpu_custom_call" | custom-call | tf_op jit(solution)/shard_map/gather_all/pallas_call | solution.py:718
  359.7 83.3 %feed_forward.1 = (f32[1536,1536]{1,0:T(8,128)}, f32[192,1536]{1,0:T(8,128)}, f32[192,1536]{1,0:T(8,128)}, f32[48,1536]{1,0:T(8,128)}) custom-call(f32[1536,1536]{1,0:T(8,128)} %bitcast.109, f32[1536,1536]{1,0:T(8,128)} %bitcast.114, f32[1536,192]{1,0:T(8,128)} %bitcast.20.refs_2_, f32[192,1536]{1,0:T(8,128)} %refs_3_.1), custom_call_target="tpu_custom_call" | custom-call | tf_op jit(solution)/shard_map/feed_forward/pallas_call | solution.py:1543
  447.4 8.0 fusion.32
  456.5 10.9 %group_gather.1 = (f32[3,4,16,1536]{3,2,1,0:T(8,128)}, f32[3,4,16,128]{3,2,1,0:T(8,128)}) custom-call(f32[3,16,1536]{2,1,0:T(8,128)} %bitcast.125, f32[3,16,128]{2,1,0:T(8,128)} %select_maximum_fusion.refs_1_), custom_call_target="tpu_custom_call" | custom-call | tf_op jit(solution)/shard_map/group_gather/pallas_call | solution.py:836
  469.8 60.4 %attend_back.1 = (f32[3,64,1536]{2,1,0:T(8,128)}, f32[1536,1536]{1,0:T(8,128)}, f32[1536,1536]{1,0:T(8,128)}, f32[48,1536]{1,0:T(8,128)}, f32[48,1536]{1,0:T(8,128)}, /*index=5*/f32[48,1536]{1,0:T(8,128)}) custom-call(s32[3,2]{1,0:T(4,128)} %compare_convert_fusion.present.refs_0_, f32[3,64,1536]{2,1,0:T(8,128)} %bitcast.120, f32[3,64,1536]{2,1,0:T(8,128)} %bitcast.129, ...), custom_call_target="tpu_custom_call" | custom-call | tf_op jit(solution)/shard_map/attend_back/pallas_call | solution.py:1266
  530.2 12.5 %group_sum.1 = f32[3,16,1536]{2,1,0:T(8,128)} custom-call(f32[3,2,2,16,1536]{4,3,2,1,0:T(8,128)} %bitcast.133), custom_call_target="tpu_custom_call" | custom-call | tf_op jit(solution)/shard_map/group_sum/pallas_call | solution.py:907
  544.5 5.3 fusion.1
  549.7 5.1 fusion.7
  554.8 127.5 %media_backward.1 = (f32[1536,1536]{1,0:T(8,128)}, f32[48,1536]{1,0:T(8,128)}, f32[8,1536]{1,0:T(8,128)}, f32[48,1536]{1,0:T(8,128)}, f32[48,1536]{1,0:T(8,128)}) custom-call(f32[1536,1536]{1,0:T(8,128)} %bitcast.108, f32[6,1,1536]{2,1,0:T(1,128)} %reshape.327.refs_1_, f32[1,1536]{1,0:T(1,128)} %get-tuple-element.202.refs_2_, ...), custom_call_target="tpu_custom_call" | custom-call | tf_op jit(solution)/shard_map/media_backward/pallas_call | solution.py:1437
  683.9 9.0 %fusion.28 = (f32[1536]{0:T(1024)S(1)}, f32[1536]{0:T(1024)S(1)}, f32[48]{0:T(128)S(1)}, f32[48,1536]{1,0:T(8,128)}) fusion(f32[3,16,1536]{2,1,0:T(8,128)} %get-tuple-element.187, f32[1536]{0:T(1024)} %copy-done.22, f32[48,1536]{1,0:T(8,128)} %get-tuple-element.85, f32[48,1536]{1,0:T(8,128)} %bitcast.124, f32[1536,1536]{1,0:T(8,128)} %bitcast.110), kind=kOutput, calls=%fused_computation.97 | convolution fusion | flops 679916480 | bytes 10635456 | tf_op jit(solution)/shard_map/dot_general | solution.py:1568
  694.9 4.4 all-to-all-start.1
  703.0 114.8 %weight_grads.1 = (f32[2,48,1536]{2,1,0:T(8,128)}, f32[16,128]{1,0:T(8,128)}) custom-call(bf16[1536,1536]{1,0:T(8,128)(2,1)} %get-tuple-element.88.xt_top, bf16[1536,1536]{1,0:T(8,128)(2,1)} %get-tuple-element.89.xt_low, bf16[1536,144]{1,0:T(8,128)(2,1)} %fusion.18.own_t, f32[1536,1536]{1,0:T(8,128)} %get-tuple-element.79.refs_3_.grad_keys, ...), custom_call_target="tpu_custom_call" | custom-call | tf_op jit(solution)/shard_map/weight_grads/pallas_call | solution.py:1358
  821.7 1.9 slice_bitcast_fusion
  824.4 2.1 copy.80
  826.5 2.8 reshape.339
  829.3 9.2 %copy.92 = f32[3,2,1,256,1536]{4,3,2,1,0:T(8,128)} copy(f32[3,2,1,256,1536]{4,3,2,1,0:T(8,128)} %bitcast.111) | data formatting | bytes 18874368
  (165 shorter events, 42.4 us)
Async XLA Ops:
  4.3 231.5 %copy-start.17 = (f32[48,6144]{1,0:T(8,128)S(1)}, f32[48,6144]{1,0:T(8,128)}, u32[]{:S(2)}) copy-start(f32[48,6144]{1,0:T(8,128)} %param.26) | copy-start | bytes 3538948
  238.6 121.1 %all-to-all-start = ((f32[48,32,192]{2,0,1:T(8,128)}), f32[48,32,192]{2,0,1:T(8,128)}, u32[]{:S(2)}, u32[]{:S(2)}) async-start(f32[48,32,192]{2,0,1:T(8,128)} %copy.73), calls=%async_computation | async-start | bytes 3145728 | tf_op jit(solution)/shard_map/all_to_all | solution.py:1614
  244.7 200.0 %copy-start.22 = (f32[1536]{0:T(1024)}, f32[1536]{0:T(1024)S(1)}, u32[]{:S(2)}) copy-start(f32[1536]{0:T(1024)S(1)} %get-tuple-element.182) | copy-start | bytes 18436
  307.8 49.4 %copy-start.29 = (f32[3,16]{1,0:T(4,128)}, f32[3,16]{1,0:T(4,128)S(1)}, u32[]{:S(2)}) copy-start(f32[3,16]{1,0:T(4,128)S(1)} %add_rsqrt_fusion.1) | copy-start | bytes 580
  309.2 50.2 %copy-start.34 = (f32[3,64]{1,0:T(4,128)S(1)}, f32[3,64]{1,0:T(4,128)}, u32[]{:S(2)}) copy-start(f32[3,64]{1,0:T(4,128)} %div.47) | copy-start | bytes 2308
  309.2 50.2 %copy-start.35 = (f32[3,64]{1,0:T(4,128)S(1)}, f32[3,64]{1,0:T(4,128)}, u32[]{:S(2)}) copy-start(f32[3,64]{1,0:T(4,128)} %rsqrt.29) | copy-start | bytes 2308
  359.6 85.0 %copy-start.28 = (f32[1536]{0:T(1024)S(1)}, f32[1536]{0:T(1024)}, u32[]{:S(2)}) copy-start(f32[1536]{0:T(1024)} %get-tuple-element.183) | copy-start | bytes 18436
  447.4 8.2 copy-start.14
  447.4 8.4 copy-start.24
  544.4 5.3 copy-start.6
  544.4 5.3 copy-start.8
  683.9 9.3 %copy-start.32 = (pred[3,2,8]{2,1,0:T(4,128)(4,1)S(1)}, pred[3,2,8]{2,1,0:T(4,128)(4,1)}, u32[]{:S(2)}) copy-start(pred[3,2,8]{2,1,0:T(4,128)(4,1)} %copy-done.31) | copy-start | bytes 148
  683.9 9.4 %copy-start.18 = (f32[192,1536]{1,0:T(8,128)S(1)}, f32[192,1536]{1,0:T(8,128)}, u32[]{:S(2)}) copy-start(f32[192,1536]{1,0:T(8,128)} %get-tuple-element.93) | copy-start | bytes 3538948
  694.9 5.4 copy-start.27
  694.9 5.5 copy-start.26
  694.9 129.6 %all-to-all-start.1 = ((f32[32,48,192]{2,1,0:T(8,128)}), f32[32,48,192]{2,1,0:T(8,128)S(1)}, u32[]{:S(2)}, u32[]{:S(2)}) async-start(f32[32,48,192]{2,1,0:T(8,128)} %bitcast.117), calls=%async_computation.1 | async-start | bytes 3145728 | tf_op jit(solution)/shard_map/all_to_all | solution.py:1648
  703.0 116.2 %copy-start.3 = (f32[3,16,1536]{2,1,0:T(8,128)S(1)}, f32[3,16,1536]{2,1,0:T(8,128)}, u32[]{:S(2)}) copy-start(f32[3,16,1536]{2,1,0:T(8,128)} %get-tuple-element.187) | copy-start | bytes 884740
  703.0 116.2 %copy-start.23 = (f32[1536]{0:T(1024)S(1)}, f32[1536]{0:T(1024)}, u32[]{:S(2)}) copy-start(f32[1536]{0:T(1024)} %copy-done.22) | copy-start | bytes 18436
  817.8 5.8 copy-start.5
  817.8 5.8 copy-start.11
  817.8 5.8 copy-start.33
  829.3 9.2 %copy-start.21 = (f32[48,1536]{1,0:T(8,128)S(1)}, f32[48,1536]{1,0:T(8,128)}, u32[]{:S(2)}) copy-start(f32[48,1536]{1,0:T(8,128)} %get-tuple-element.232) | copy-start | bytes 884740
  829.3 9.9 %copy-start.20 = (f32[48,1536]{1,0:T(8,128)S(1)}, f32[48,1536]{1,0:T(8,128)}, u32[]{:S(2)}) copy-start(f32[48,1536]{1,0:T(8,128)} %get-tuple-element.235) | copy-start | bytes 884740
  829.3 10.6 %copy-start.16 = (f32[192,1536]{1,0:T(8,128)S(1)}, f32[192,1536]{1,0:T(8,128)}, u32[]{:S(2)}) copy-start(f32[192,1536]{1,0:T(8,128)} %get-tuple-element.237) | copy-start | bytes 3538948
  (15 other events, 39.3 us)

commit v2 on v1

--- a/solution.py
+++ b/solution.py
@@ -489,9 +489,6 @@
         return (self.own, self.along_z, self.across, self.corner)
 
 
-LAG = 2
-
-
 def waves_of(plan, ahead):
     first, *stages = plan.stages()
     count, last, lag = plan.count, len(stages) - 1, plan.lag
@@ -499,7 +496,7 @@
     waves = [[functools.partial(first, p) for p in range(ahead)]]
     for t in range(count + last * lag):
         wave = [functools.partial(first, t + ahead)] if t + ahead < count else []
-        order = range(last, -1, -1)
+        order = range(last + 1)
         waves.append(wave + [functools.partial(stages[s], t - s * lag) for s in order if 0 <= t - s * lag < count])
     return waves
 
@@ -510,7 +507,7 @@
 
 
 class Scatter:
-    lag = LAG
+    lag = 1
 
     def __init__(self, here, count, mine, theirs, load, out, scratch):
         self.here, self.count, self.mine, self.theirs, self.load, self.out = here, count, mine, theirs, load, out
@@ -1320,8 +1317,8 @@
             mats[2 * n + w, pl.ds(i * 2, 2)] = made.reshape((2, 2, 2, 2, 48, cut))
 
         sums.start(2 * n + w)
-        for s in (4, 3, 2, 1):
-            p = 2 * n + w - LAG * s
+        for s in (1, 2, 3, 4):
+            p = 2 * n + w - s
 
             @pl.when(p >= 0)
             def _():
@@ -1336,10 +1333,10 @@
 
     @pl.when(n == steps - 1)
     def _():
-        for t in range(2 * steps, 2 * steps + 4 * LAG):
-            for s in (4, 3, 2, 1):
-                if 0 <= t - LAG * s < 2 * steps:
-                    stages[s](t - LAG * s)
+        for t in range(2 * steps, 2 * steps + 4):
+            for s in (1, 2, 3, 4):
+                if t - s < 2 * steps:
+                    stages[s](t - s)
 
         @pl.loop(0, 2 * steps)
         def _(p):

time: 850 us -> 858 us (level)
  transfers between devices with their start and end apart: 2 -> 2, of which waited for: 0 -> 0; matrix products, arithmetic and copies ran while one was open for 4% -> 4% of each run, Pallas kernels for 25% -> 24%
where the time goes in v2:
time: 858 us; the launch traced here: 849 us
  Pallas kernels  741 us (86%)
  local copies, waits for them, and re-layouts  45.3 us (5%)
  matrix products  34.2 us (4%)
  other arithmetic  18.8 us (2%)
    pallas_call x1, Pallas kernels, opening(): pl.pallas_call(functools.partial(opening_kernel, cuts), grid=(slots + 2 *...  231 us
    pallas_call x1, Pallas kernels, media_backward(): pl.pallas_call(functools.partial(media_back_kernel, plan, steps), grid=(s...  134 us
    pallas_call x1, Pallas kernels, weight_grads(): pl.pallas_call(functools.partial(weight_kernel, steps), grid=(steps,), in...  111 us
    pallas_call x1, Pallas kernels, feed_forward(): pl.pallas_call(functools.partial(feed_kernel, blocks), grid=(2 * blocks,)...  82.3 us
    pallas_call x1, Pallas kernels, attend_back(): pl.pallas_call(functools.partial(attend_back_kernel, 1.0 / math.sqrt(head...  63.6 us
    pallas_call x1, Pallas kernels, gather_all(): pl.pallas_call(functools.partial(gather_kernel, count, cuts), out_shape=f...  51 us
    pallas_call x1, Pallas kernels, attend(): pl.pallas_call(functools.partial(attend_kernel, 1.0 / math.sqrt(head), he...  27.2 us
  transfers between devices with their start and end apart: 2, of which 0 were waited for; matrix products, arithmetic and copies ran while one was open for 4% of the time, Pallas kernels for 24%

profile of v2, /device:TPU:0, one launch (start us, length us, event | category | flops | bytes accessed | tf_op | source)
XLA Modules:
  0.0 849.2 jit_solution(12985429313943594701)
XLA Ops:
  4.3 231.4 %opening.1 = (f32[16,1536]{1,0:T(8,128)}, f32[1536,1536]{1,0:T(8,128)}, f32[1536,1536]{1,0:T(8,128)}, f32[48,1536]{1,0:T(8,128)}, f32[48,1536]{1,0:T(8,128)}, /*...) custom-call(s32[6]{0:T(128)} %reshape.300.refs_0_, ...), custom_call_target="tpu_custom_call" | custom-call | tf_op jit(solution)/shard_map/opening/pallas_call | solution.py:1098
  236.4 2.1 copy.73
  238.5 3.8 all-to-all-start
  246.0 27.2 %attend.1 = (f32[3,64,1536]{2,1,0:T(8,128)}, f32[3,8,128]{2,1,0:T(8,128)}, f32[3,8,128]{2,1,0:T(8,128)}) custom-call(s32[3,2]{1,0:T(4,128)} %compare_convert_fusion.present.refs_0_, f32[3,64,1536]{2,1,0:T(8,128)} %bitcast.119, f32[1536,1536]{1,0:T(8,128)} %get-tuple-element.58.keys.refs_5_, f32[1536,1536]{1,0:T(8,128)} %get-tuple-element.59.values.refs_6_, ...), custom_call_target="tpu_custom_call" | custom-call | tf_op jit(solution)/shard_map/attend/pallas_call | solution.py:1212
  275.7 17.1 %group_swap.1 = (f32[3,4,16,1536]{3,2,1,0:T(8,128)}, f32[3,4,16,128]{3,2,1,0:T(8,128)}) custom-call(f32[3,4,16,1536]{3,2,1,0:T(8,128)} %bitcast.132, f32[3,4,16,128]{3,2,1,0:T(8,128)} %bitcast.135), custom_call_target="tpu_custom_call" | custom-call | tf_op jit(solution)/shard_map/group_swap/pallas_call | solution.py:871
  296.3 1.8 mul.147
  298.0 1.8 multiply_reduce_fusion.1
  300.8 6.8 fusion.31
  309.1 51.0 %gather_all.1 = f32[4,2,2,2,48,1536]{5,4,3,2,1,0:T(8,128)} custom-call(f32[48,1536]{1,0:T(8,128)} %bitcast.130), custom_call_target="tpu_custom_call" | custom-call | tf_op jit(solution)/shard_map/gather_all/pallas_call | solution.py:715
  362.6 82.3 %feed_forward.1 = (f32[1536,1536]{1,0:T(8,128)}, f32[192,1536]{1,0:T(8,128)}, f32[192,1536]{1,0:T(8,128)}, f32[48,1536]{1,0:T(8,128)}) custom-call(f32[1536,1536]{1,0:T(8,128)} %bitcast.109, f32[1536,1536]{1,0:T(8,128)} %bitcast.114, f32[1536,192]{1,0:T(8,128)} %bitcast.20.refs_2_, f32[192,1536]{1,0:T(8,128)} %refs_3_.1), custom_call_target="tpu_custom_call" | custom-call | tf_op jit(solution)/shard_map/feed_forward/pallas_call | solution.py:1540
  449.3 8.0 fusion.32
  458.4 11.5 %group_gather.1 = (f32[3,4,16,1536]{3,2,1,0:T(8,128)}, f32[3,4,16,128]{3,2,1,0:T(8,128)}) custom-call(f32[3,16,1536]{2,1,0:T(8,128)} %bitcast.125, f32[3,16,128]{2,1,0:T(8,128)} %select_maximum_fusion.refs_1_), custom_call_target="tpu_custom_call" | custom-call | tf_op jit(solution)/shard_map/group_gather/pallas_call | solution.py:833
  472.3 63.6 %attend_back.1 = (f32[3,64,1536]{2,1,0:T(8,128)}, f32[1536,1536]{1,0:T(8,128)}, f32[1536,1536]{1,0:T(8,128)}, f32[48,1536]{1,0:T(8,128)}, f32[48,1536]{1,0:T(8,128)}, /*index=5*/f32[48,1536]{1,0:T(8,128)}) custom-call(s32[3,2]{1,0:T(4,128)} %compare_convert_fusion.present.refs_0_, f32[3,64,1536]{2,1,0:T(8,128)} %bitcast.120, f32[3,64,1536]{2,1,0:T(8,128)} %bitcast.129, ...), custom_call_target="tpu_custom_call" | custom-call | tf_op jit(solution)/shard_map/attend_back/pallas_call | solution.py:1263
  535.9 11.6 %group_sum.1 = f32[3,16,1536]{2,1,0:T(8,128)} custom-call(f32[3,2,2,16,1536]{4,3,2,1,0:T(8,128)} %bitcast.133), custom_call_target="tpu_custom_call" | custom-call | tf_op jit(solution)/shard_map/group_sum/pallas_call | solution.py:904
  549.2 5.3 fusion.1
  554.5 5.1 fusion.7
  559.5 133.9 %media_backward.1 = (f32[1536,1536]{1,0:T(8,128)}, f32[48,1536]{1,0:T(8,128)}, f32[8,1536]{1,0:T(8,128)}, f32[48,1536]{1,0:T(8,128)}, f32[48,1536]{1,0:T(8,128)}) custom-call(f32[1536,1536]{1,0:T(8,128)} %bitcast.108, f32[6,1,1536]{2,1,0:T(1,128)} %reshape.327.refs_1_, f32[1,1536]{1,0:T(1,128)} %get-tuple-element.202.refs_2_, ...), custom_call_target="tpu_custom_call" | custom-call | tf_op jit(solution)/shard_map/media_backward/pallas_call | solution.py:1434
  695.1 9.0 %fusion.28 = (f32[1536]{0:T(1024)S(1)}, f32[1536]{0:T(1024)S(1)}, f32[48]{0:T(128)S(1)}, f32[48,1536]{1,0:T(8,128)}) fusion(f32[3,16,1536]{2,1,0:T(8,128)} %get-tuple-element.187, f32[1536]{0:T(1024)} %copy-done.22, f32[48,1536]{1,0:T(8,128)} %get-tuple-element.85, f32[48,1536]{1,0:T(8,128)} %bitcast.124, f32[1536,1536]{1,0:T(8,128)} %bitcast.110), kind=kOutput, calls=%fused_computation.97 | convolution fusion | flops 679916480 | bytes 10635456 | tf_op jit(solution)/shard_map/dot_general | solution.py:1565
  706.1 4.5 all-to-all-start.1
  714.2 111.4 %weight_grads.1 = (f32[2,48,1536]{2,1,0:T(8,128)}, f32[16,128]{1,0:T(8,128)}) custom-call(bf16[1536,1536]{1,0:T(8,128)(2,1)} %get-tuple-element.88.xt_top, bf16[1536,1536]{1,0:T(8,128)(2,1)} %get-tuple-element.89.xt_low, bf16[1536,144]{1,0:T(8,128)(2,1)} %fusion.18.own_t, f32[1536,1536]{1,0:T(8,128)} %get-tuple-element.79.refs_3_.grad_keys, ...), custom_call_target="tpu_custom_call" | custom-call | tf_op jit(solution)/shard_map/weight_grads/pallas_call | solution.py:1355
  829.6 1.9 slice_bitcast_fusion
  832.3 2.1 copy.80
  834.4 2.8 reshape.339
  837.2 9.2 %copy.92 = f32[3,2,1,256,1536]{4,3,2,1,0:T(8,128)} copy(f32[3,2,1,256,1536]{4,3,2,1,0:T(8,128)} %bitcast.111) | data formatting | bytes 18874368
  (165 shorter events, 42.4 us)
Async XLA Ops:
  4.3 231.4 %copy-start.17 = (f32[48,6144]{1,0:T(8,128)S(1)}, f32[48,6144]{1,0:T(8,128)}, u32[]{:S(2)}) copy-start(f32[48,6144]{1,0:T(8,128)} %param.26) | copy-start | bytes 3538948
  238.5 124.1 %all-to-all-start = ((f32[48,32,192]{2,0,1:T(8,128)}), f32[48,32,192]{2,0,1:T(8,128)}, u32[]{:S(2)}, u32[]{:S(2)}) async-start(f32[48,32,192]{2,0,1:T(8,128)} %copy.73), calls=%async_computation | async-start | bytes 3145728 | tf_op jit(solution)/shard_map/all_to_all | solution.py:1611
  244.6 202.0 %copy-start.22 = (f32[1536]{0:T(1024)}, f32[1536]{0:T(1024)S(1)}, u32[]{:S(2)}) copy-start(f32[1536]{0:T(1024)S(1)} %get-tuple-element.182) | copy-start | bytes 18436
  307.7 52.4 %copy-start.29 = (f32[3,16]{1,0:T(4,128)}, f32[3,16]{1,0:T(4,128)S(1)}, u32[]{:S(2)}) copy-start(f32[3,16]{1,0:T(4,128)S(1)} %add_rsqrt_fusion.1) | copy-start | bytes 580
  309.1 53.2 %copy-start.34 = (f32[3,64]{1,0:T(4,128)S(1)}, f32[3,64]{1,0:T(4,128)}, u32[]{:S(2)}) copy-start(f32[3,64]{1,0:T(4,128)} %div.47) | copy-start | bytes 2308
  309.1 53.3 %copy-start.35 = (f32[3,64]{1,0:T(4,128)S(1)}, f32[3,64]{1,0:T(4,128)}, u32[]{:S(2)}) copy-start(f32[3,64]{1,0:T(4,128)} %rsqrt.29) | copy-start | bytes 2308
  362.6 84.1 %copy-start.28 = (f32[1536]{0:T(1024)S(1)}, f32[1536]{0:T(1024)}, u32[]{:S(2)}) copy-start(f32[1536]{0:T(1024)} %get-tuple-element.183) | copy-start | bytes 18436
  449.3 8.2 copy-start.14
  449.3 8.4 copy-start.24
  549.2 5.3 copy-start.6
  549.2 5.3 copy-start.8
  695.1 9.3 %copy-start.32 = (pred[3,2,8]{2,1,0:T(4,128)(4,1)S(1)}, pred[3,2,8]{2,1,0:T(4,128)(4,1)}, u32[]{:S(2)}) copy-start(pred[3,2,8]{2,1,0:T(4,128)(4,1)} %copy-done.31) | copy-start | bytes 148
  695.1 9.4 %copy-start.18 = (f32[192,1536]{1,0:T(8,128)S(1)}, f32[192,1536]{1,0:T(8,128)}, u32[]{:S(2)}) copy-start(f32[192,1536]{1,0:T(8,128)} %get-tuple-element.93) | copy-start | bytes 3538948
  706.1 5.4 copy-start.27
  706.1 5.5 copy-start.26
  706.1 126.2 %all-to-all-start.1 = ((f32[32,48,192]{2,1,0:T(8,128)}), f32[32,48,192]{2,1,0:T(8,128)S(1)}, u32[]{:S(2)}, u32[]{:S(2)}) async-start(f32[32,48,192]{2,1,0:T(8,128)} %bitcast.117), calls=%async_computation.1 | async-start | bytes 3145728 | tf_op jit(solution)/shard_map/all_to_all | solution.py:1645
  714.2 112.8 %copy-start.3 = (f32[3,16,1536]{2,1,0:T(8,128)S(1)}, f32[3,16,1536]{2,1,0:T(8,128)}, u32[]{:S(2)}) copy-start(f32[3,16,1536]{2,1,0:T(8,128)} %get-tuple-element.187) | copy-start | bytes 884740
  714.2 112.8 %copy-start.23 = (f32[1536]{0:T(1024)S(1)}, f32[1536]{0:T(1024)}, u32[]{:S(2)}) copy-start(f32[1536]{0:T(1024)} %copy-done.22) | copy-start | bytes 18436
  825.7 5.8 copy-start.5
  825.7 5.8 copy-start.11
  825.7 5.8 copy-start.33
  837.2 9.2 %copy-start.21 = (f32[48,1536]{1,0:T(8,128)S(1)}, f32[48,1536]{1,0:T(8,128)}, u32[]{:S(2)}) copy-start(f32[48,1536]{1,0:T(8,128)} %get-tuple-element.232) | copy-start | bytes 884740
  837.2 9.9 %copy-start.20 = (f32[48,1536]{1,0:T(8,128)S(1)}, f32[48,1536]{1,0:T(8,128)}, u32[]{:S(2)}) copy-start(f32[48,1536]{1,0:T(8,128)} %get-tuple-element.235) | copy-start | bytes 884740
  837.2 10.6 %copy-start.16 = (f32[192,1536]{1,0:T(8,128)S(1)}, f32[192,1536]{1,0:T(8,128)}, u32[]{:S(2)}) copy-start(f32[192,1536]{1,0:T(8,128)} %get-tuple-element.237) | copy-start | bytes 3538948
  (15 other events, 39.4 us)

commit v3 on v2

--- a/solution.py
+++ b/solution.py
@@ -489,6 +489,9 @@
         return (self.own, self.along_z, self.across, self.corner)
 
 
+LAG = 2
+
+
 def waves_of(plan, ahead):
     first, *stages = plan.stages()
     count, last, lag = plan.count, len(stages) - 1, plan.lag
@@ -496,7 +499,7 @@
     waves = [[functools.partial(first, p) for p in range(ahead)]]
     for t in range(count + last * lag):
         wave = [functools.partial(first, t + ahead)] if t + ahead < count else []
-        order = range(last + 1)
+        order = range(last, -1, -1)
         waves.append(wave + [functools.partial(stages[s], t - s * lag) for s in order if 0 <= t - s * lag < count])
     return waves
 
@@ -507,7 +510,7 @@
 
 
 class Scatter:
-    lag = 1
+    lag = LAG
 
     def __init__(self, here, count, mine, theirs, load, out, scratch):
         self.here, self.count, self.mine, self.theirs, self.load, self.out = here, count, mine, theirs, load, out
@@ -1020,9 +1023,12 @@
 
     pl.when(step == 0)(start)
     at_step = {2: 2, 4: 3, 5: 4, slots + 1: 5, slots + 2: 6, slots + 4: 7, slots + 5: 8}
-    at_step.update({slots + chunks + i: 8 + i for i in range(1, 5)})
-    for s, w in at_step.items():
-        pl.when(step == s)(functools.partial(run, waves[w]))
+    ending, late = len(waves) - 9, slots + chunks + 1
+    at_step = {s: waves[w] for s, w in at_step.items()}
+    for i in range(5):
+        at_step[late + i] = sum(waves[9 + ending * i // 5 : 9 + ending * (i + 1) // 5], [])
+    for s, wave in at_step.items():
+        pl.when(step == s)(functools.partial(run, wave))
 
     @pl.when(step < slots)
     def _():
@@ -1090,7 +1096,8 @@
     chunks = width // cut
     shards = [packed, key_w, value_w, query_w, cot, out_w]
     cuts = [(a, lo, lo + WIDE) for lo in range(0, width, WIDE) for a in (0, 1)]
-    cuts += [(a, lo, lo + WIDE) for a in (2, 3, 4) for lo in range(0, width, WIDE)]
+    cuts += [(a, lo, lo + WIDE) for a in (2, 3) for lo in range(0, width, WIDE)]
+    cuts += [(4, lo, lo + cut) for lo in range(0, width, cut)]
     clip = lambda i, lo: jnp.clip(i - lo, 0, chunks - 1)
     chunk_of = lambda n, lo: pl.BlockSpec((n, cut), lambda i: (0, clip(i, lo)))
     turned = pl.BlockSpec((width, BLOCK), lambda i: (0, jnp.minimum(i, slots - 1)))

time: 858 us -> 850 us (level)
  Pallas kernels: 741 us -> 732 us
where the time goes in v3:
time: 850 us; the launch traced here: 841 us
  Pallas kernels  732 us (86%)
  local copies, waits for them, and re-layouts  45.3 us (5%)
  matrix products  34.1 us (4%)
  other arithmetic  18.8 us (2%)
  starting transfers between devices  9.1 us (1%)
    pallas_call x1, Pallas kernels, opening(): pl.pallas_call(functools.partial(opening_kernel, cuts), grid=(slots + 2 *...  233 us
    pallas_call x1, Pallas kernels, media_backward(): pl.pallas_call(functools.partial(media_back_kernel, plan, steps), grid=(s...  128 us
    pallas_call x1, Pallas kernels, weight_grads(): pl.pallas_call(functools.partial(weight_kernel, steps), grid=(steps,), in...  111 us
    pallas_call x1, Pallas kernels, feed_forward(): pl.pallas_call(functools.partial(feed_kernel, blocks), grid=(2 * blocks,)...  83.4 us
    pallas_call x1, Pallas kernels, attend_back(): pl.pallas_call(functools.partial(attend_back_kernel, 1.0 / math.sqrt(head...  60.2 us
    pallas_call x1, Pallas kernels, gather_all(): pl.pallas_call(functools.partial(gather_kernel, count, cuts), out_shape=f...  48 us
    pallas_call x1, Pallas kernels, attend(): pl.pallas_call(functools.partial(attend_kernel, 1.0 / math.sqrt(head), he...  27.2 us
    pallas_call x1, Pallas kernels, group_swap(): pl.pallas_call(functools.partial(group_swap_kernel, count), out_shape=[ja...  17.1 us
  transfers between devices with their start and end apart: 2, of which 0 were waited for; matrix products, arithmetic and copies ran while one was open for 4% of the time, Pallas kernels for 24%

profile of v3, /device:TPU:0, one launch (start us, length us, event | category | flops | bytes accessed | tf_op | source)
XLA Modules:
  0.0 840.8 jit_solution(464922944411990473)
XLA Ops:
  4.3 233.4 %opening.1 = (f32[16,1536]{1,0:T(8,128)}, f32[1536,1536]{1,0:T(8,128)}, f32[1536,1536]{1,0:T(8,128)}, f32[48,1536]{1,0:T(8,128)}, f32[48,1536]{1,0:T(8,128)}, /*...) custom-call(s32[6]{0:T(128)} %reshape.300.refs_0_, ...), custom_call_target="tpu_custom_call" | custom-call | tf_op jit(solution)/shard_map/opening/pallas_call | solution.py:1105
  238.4 2.1 copy.73
  240.5 4.7 all-to-all-start
  248.9 27.2 %attend.1 = (f32[3,64,1536]{2,1,0:T(8,128)}, f32[3,8,128]{2,1,0:T(8,128)}, f32[3,8,128]{2,1,0:T(8,128)}) custom-call(s32[3,2]{1,0:T(4,128)} %compare_convert_fusion.present.refs_0_, f32[3,64,1536]{2,1,0:T(8,128)} %bitcast.119, f32[1536,1536]{1,0:T(8,128)} %get-tuple-element.58.keys.refs_5_, f32[1536,1536]{1,0:T(8,128)} %get-tuple-element.59.values.refs_6_, ...), custom_call_target="tpu_custom_call" | custom-call | tf_op jit(solution)/shard_map/attend/pallas_call | solution.py:1219
  278.6 17.1 %group_swap.1 = (f32[3,4,16,1536]{3,2,1,0:T(8,128)}, f32[3,4,16,128]{3,2,1,0:T(8,128)}) custom-call(f32[3,4,16,1536]{3,2,1,0:T(8,128)} %bitcast.132, f32[3,4,16,128]{3,2,1,0:T(8,128)} %bitcast.135), custom_call_target="tpu_custom_call" | custom-call | tf_op jit(solution)/shard_map/group_swap/pallas_call | solution.py:874
  299.1 1.8 mul.147
  300.9 1.8 multiply_reduce_fusion.1
  303.6 6.8 fusion.31
  311.9 48.0 %gather_all.1 = f32[4,2,2,2,48,1536]{5,4,3,2,1,0:T(8,128)} custom-call(f32[48,1536]{1,0:T(8,128)} %bitcast.130), custom_call_target="tpu_custom_call" | custom-call | tf_op jit(solution)/shard_map/gather_all/pallas_call | solution.py:718
  362.4 83.4 %feed_forward.1 = (f32[1536,1536]{1,0:T(8,128)}, f32[192,1536]{1,0:T(8,128)}, f32[192,1536]{1,0:T(8,128)}, f32[48,1536]{1,0:T(8,128)}) custom-call(f32[1536,1536]{1,0:T(8,128)} %bitcast.109, f32[1536,1536]{1,0:T(8,128)} %bitcast.114, f32[1536,192]{1,0:T(8,128)} %bitcast.20.refs_2_, f32[192,1536]{1,0:T(8,128)} %refs_3_.1), custom_call_target="tpu_custom_call" | custom-call | tf_op jit(solution)/shard_map/feed_forward/pallas_call | solution.py:1547
  450.3 8.0 fusion.32
  459.4 10.9 %group_gather.1 = (f32[3,4,16,1536]{3,2,1,0:T(8,128)}, f32[3,4,16,128]{3,2,1,0:T(8,128)}) custom-call(f32[3,16,1536]{2,1,0:T(8,128)} %bitcast.125, f32[3,16,128]{2,1,0:T(8,128)} %select_maximum_fusion.refs_1_), custom_call_target="tpu_custom_call" | custom-call | tf_op jit(solution)/shard_map/group_gather/pallas_call | solution.py:836
  472.7 60.2 %attend_back.1 = (f32[3,64,1536]{2,1,0:T(8,128)}, f32[1536,1536]{1,0:T(8,128)}, f32[1536,1536]{1,0:T(8,128)}, f32[48,1536]{1,0:T(8,128)}, f32[48,1536]{1,0:T(8,128)}, /*index=5*/f32[48,1536]{1,0:T(8,128)}) custom-call(s32[3,2]{1,0:T(4,128)} %compare_convert_fusion.present.refs_0_, f32[3,64,1536]{2,1,0:T(8,128)} %bitcast.120, f32[3,64,1536]{2,1,0:T(8,128)} %bitcast.129, ...), custom_call_target="tpu_custom_call" | custom-call | tf_op jit(solution)/shard_map/attend_back/pallas_call | solution.py:1270
  532.9 12.5 %group_sum.1 = f32[3,16,1536]{2,1,0:T(8,128)} custom-call(f32[3,2,2,16,1536]{4,3,2,1,0:T(8,128)} %bitcast.133), custom_call_target="tpu_custom_call" | custom-call | tf_op jit(solution)/shard_map/group_sum/pallas_call | solution.py:907
  547.1 5.3 fusion.1
  552.4 5.1 fusion.7
  557.5 127.5 %media_backward.1 = (f32[1536,1536]{1,0:T(8,128)}, f32[48,1536]{1,0:T(8,128)}, f32[8,1536]{1,0:T(8,128)}, f32[48,1536]{1,0:T(8,128)}, f32[48,1536]{1,0:T(8,128)}) custom-call(f32[1536,1536]{1,0:T(8,128)} %bitcast.108, f32[6,1,1536]{2,1,0:T(1,128)} %reshape.327.refs_1_, f32[1,1536]{1,0:T(1,128)} %get-tuple-element.202.refs_2_, ...), custom_call_target="tpu_custom_call" | custom-call | tf_op jit(solution)/shard_map/media_backward/pallas_call | solution.py:1441
  686.6 9.0 %fusion.28 = (f32[1536]{0:T(1024)S(1)}, f32[1536]{0:T(1024)S(1)}, f32[48]{0:T(128)S(1)}, f32[48,1536]{1,0:T(8,128)}) fusion(f32[3,16,1536]{2,1,0:T(8,128)} %get-tuple-element.187, f32[1536]{0:T(1024)} %copy-done.22, f32[48,1536]{1,0:T(8,128)} %get-tuple-element.85, f32[48,1536]{1,0:T(8,128)} %bitcast.124, f32[1536,1536]{1,0:T(8,128)} %bitcast.110), kind=kOutput, calls=%fused_computation.97 | convolution fusion | flops 679916480 | bytes 10635456 | tf_op jit(solution)/shard_map/dot_general | solution.py:1572
  697.6 4.4 all-to-all-start.1
  705.7 111.4 %weight_grads.1 = (f32[2,48,1536]{2,1,0:T(8,128)}, f32[16,128]{1,0:T(8,128)}) custom-call(bf16[1536,1536]{1,0:T(8,128)(2,1)} %get-tuple-element.88.xt_top, bf16[1536,1536]{1,0:T(8,128)(2,1)} %get-tuple-element.89.xt_low, bf16[1536,144]{1,0:T(8,128)(2,1)} %fusion.18.own_t, f32[1536,1536]{1,0:T(8,128)} %get-tuple-element.79.refs_3_.grad_keys, ...), custom_call_target="tpu_custom_call" | custom-call | tf_op jit(solution)/shard_map/weight_grads/pallas_call | solution.py:1362
  821.1 1.9 slice_bitcast_fusion
  823.8 2.1 copy.80
  825.9 2.8 reshape.339
  828.7 9.2 %copy.92 = f32[3,2,1,256,1536]{4,3,2,1,0:T(8,128)} copy(f32[3,2,1,256,1536]{4,3,2,1,0:T(8,128)} %bitcast.111) | data formatting | bytes 18874368
  (165 shorter events, 42.4 us)
Async XLA Ops:
  4.3 233.4 %copy-start.17 = (f32[48,6144]{1,0:T(8,128)S(1)}, f32[48,6144]{1,0:T(8,128)}, u32[]{:S(2)}) copy-start(f32[48,6144]{1,0:T(8,128)} %param.26) | copy-start | bytes 3538948
  240.5 122.0 %all-to-all-start = ((f32[48,32,192]{2,0,1:T(8,128)}), f32[48,32,192]{2,0,1:T(8,128)}, u32[]{:S(2)}, u32[]{:S(2)}) async-start(f32[48,32,192]{2,0,1:T(8,128)} %copy.73), calls=%async_computation | async-start | bytes 3145728 | tf_op jit(solution)/shard_map/all_to_all | solution.py:1618
  247.4 200.2 %copy-start.22 = (f32[1536]{0:T(1024)}, f32[1536]{0:T(1024)S(1)}, u32[]{:S(2)}) copy-start(f32[1536]{0:T(1024)S(1)} %get-tuple-element.182) | copy-start | bytes 18436
  310.6 49.4 %copy-start.29 = (f32[3,16]{1,0:T(4,128)}, f32[3,16]{1,0:T(4,128)S(1)}, u32[]{:S(2)}) copy-start(f32[3,16]{1,0:T(4,128)S(1)} %add_rsqrt_fusion.1) | copy-start | bytes 580
  311.9 50.3 %copy-start.34 = (f32[3,64]{1,0:T(4,128)S(1)}, f32[3,64]{1,0:T(4,128)}, u32[]{:S(2)}) copy-start(f32[3,64]{1,0:T(4,128)} %div.47) | copy-start | bytes 2308
  311.9 50.3 %copy-start.35 = (f32[3,64]{1,0:T(4,128)S(1)}, f32[3,64]{1,0:T(4,128)}, u32[]{:S(2)}) copy-start(f32[3,64]{1,0:T(4,128)} %rsqrt.29) | copy-start | bytes 2308
  362.4 85.2 %copy-start.28 = (f32[1536]{0:T(1024)S(1)}, f32[1536]{0:T(1024)}, u32[]{:S(2)}) copy-start(f32[1536]{0:T(1024)} %get-tuple-element.183) | copy-start | bytes 18436
  450.3 8.2 copy-start.14
  450.3 8.4 copy-start.24
  547.1 5.3 copy-start.6
  547.1 5.3 copy-start.8
  686.6 9.3 %copy-start.32 = (pred[3,2,8]{2,1,0:T(4,128)(4,1)S(1)}, pred[3,2,8]{2,1,0:T(4,128)(4,1)}, u32[]{:S(2)}) copy-start(pred[3,2,8]{2,1,0:T(4,128)(4,1)} %copy-done.31) | copy-start | bytes 148
  686.6 9.4 %copy-start.18 = (f32[192,1536]{1,0:T(8,128)S(1)}, f32[192,1536]{1,0:T(8,128)}, u32[]{:S(2)}) copy-start(f32[192,1536]{1,0:T(8,128)} %get-tuple-element.93) | copy-start | bytes 3538948
  697.6 5.4 copy-start.27
  697.6 5.5 copy-start.26
  697.6 126.2 %all-to-all-start.1 = ((f32[32,48,192]{2,1,0:T(8,128)}), f32[32,48,192]{2,1,0:T(8,128)S(1)}, u32[]{:S(2)}, u32[]{:S(2)}) async-start(f32[32,48,192]{2,1,0:T(8,128)} %bitcast.117), calls=%async_computation.1 | async-start | bytes 3145728 | tf_op jit(solution)/shard_map/all_to_all | solution.py:1652
  705.7 112.8 %copy-start.3 = (f32[3,16,1536]{2,1,0:T(8,128)S(1)}, f32[3,16,1536]{2,1,0:T(8,128)}, u32[]{:S(2)}) copy-start(f32[3,16,1536]{2,1,0:T(8,128)} %get-tuple-element.187) | copy-start | bytes 884740
  705.7 112.8 %copy-start.23 = (f32[1536]{0:T(1024)S(1)}, f32[1536]{0:T(1024)}, u32[]{:S(2)}) copy-start(f32[1536]{0:T(1024)} %copy-done.22) | copy-start | bytes 18436
  817.2 5.8 copy-start.5
  817.2 5.8 copy-start.11
  817.2 5.8 copy-start.33
  828.7 9.2 %copy-start.21 = (f32[48,1536]{1,0:T(8,128)S(1)}, f32[48,1536]{1,0:T(8,128)}, u32[]{:S(2)}) copy-start(f32[48,1536]{1,0:T(8,128)} %get-tuple-element.232) | copy-start | bytes 884740
  828.7 9.9 %copy-start.20 = (f32[48,1536]{1,0:T(8,128)S(1)}, f32[48,1536]{1,0:T(8,128)}, u32[]{:S(2)}) copy-start(f32[48,1536]{1,0:T(8,128)} %get-tuple-element.235) | copy-start | bytes 884740
  828.7 10.6 %copy-start.16 = (f32[192,1536]{1,0:T(8,128)S(1)}, f32[192,1536]{1,0:T(8,128)}, u32[]{:S(2)}) copy-start(f32[192,1536]{1,0:T(8,128)} %get-tuple-element.237) | copy-start | bytes 3538948
  (15 other events, 40.2 us)
